TPU v7x, 256 devices: a whole 4x4x8 slice. The times are simulated.
256 devices in a mesh: node: 8 (over y, core), local: 32 (over z, x).
Axes of the slice: x: 4, y: 4, z: 8, core: 2. Of those that a mesh axis runs over, the one named last changes fastest.
Arguments:
- grad_out: bfloat16 [32768, 3584], P(('node', 'local')), may hold values from -24 to 24
- expert_ids: int32 [32768, 8], P(('node', 'local')), may hold values from 0 to 127, as said below
- gate_probs: bfloat16 [32768, 8], P(('node', 'local')), may hold values from 0.099609375 to 1
- down_weight: bfloat16 [131072, 3584], P(('node', 'local')), may hold values from -0.046875 to 0.046875
- hidden_act: bfloat16 [2048, 131072], P(None, ('node', 'local')), may hold values from -32 to 32
Outputs:
- clipped_grad: bfloat16 [131072, 3584], P(('node', 'local'))
- hidden_grad: bfloat16 [2048, 131072], P(None, ('node', 'local'))
- router_grad: float32 [32768, 8], P(('node', 'local'))
Inputs may be any that keep to these rules, and one draw needn't show every extreme that they name: `expert_ids`: each token names 8 different experts, two in each of 4 different groups, where expert e lies in group e // 16; each aligned block of 128 tokens names every expert exactly 8 times, so every expert has exactly 2048 rows.
All inputs are finite; a program needn't handle non-finite values.
Results may differ from a plain program's by a relative error of at most 0.0049.
Values may be sent and summed in bfloat16 or wider, within the bound.
A program may use at most 128 MiB of HBM per device.

v0:
```python
import jax
import jax.numpy as jnp
from jax import lax
from jax.sharding import PartitionSpec as P

TOP = 8
TOK_DEV = 128
SLOTS = 2048


clip_rms = 0.25
square_eps = 1e-06


def both_halves(row_block, node_count, per_node, per_source):
    trailing = row_block.shape[2:]
    shaped = row_block.reshape((node_count, per_node, 1, per_source) + trailing)
    widened = jnp.broadcast_to(shaped, (node_count, per_node, 2, per_source) + trailing)
    return widened.reshape((node_count, 2 * per_node, per_source) + trailing)


def per_device(grad_out, expert_ids, gate_probs, down_weight, hidden_act):
    node_count = lax.axis_size("node")
    local_count = lax.axis_size("local")
    per_node = local_count // 2
    experts_all = node_count * per_node
    routes_dev = TOK_DEV * TOP
    per_source = routes_dev // experts_all
    flat_ids = expert_ids.reshape(routes_dev)
    onehot = (flat_ids[:, None] == jnp.arange(experts_all, dtype=jnp.int32)[None, :]).astype(
        jnp.int32
    )
    rank_of = jnp.sum(jnp.cumsum(onehot, axis=0) * onehot, axis=1) - 1
    target = flat_ids * per_source + rank_of
    route_ids = jnp.arange(routes_dev, dtype=jnp.int32)
    sorted_routes = jnp.zeros((routes_dev,), jnp.int32).at[target].set(route_ids)
    gates_sorted = gate_probs.reshape(routes_dev)[sorted_routes]
    gate_block = gates_sorted.reshape(node_count, per_node * per_source)
    send_rows = grad_out[sorted_routes // TOP].reshape(
        node_count, per_node * per_source, grad_out.shape[1]
    )
    rows_in, gates_in = (
        lax.all_to_all(
            lax.all_to_all(
                both_halves(send_rows, node_count, per_node, per_source),
                "node",
                split_axis=0,
                concat_axis=0,
                tiled=True,
            ),
            "local",
            split_axis=1,
            concat_axis=1,
            tiled=True,
        ),
        lax.all_to_all(
            lax.all_to_all(
                both_halves(gate_block, node_count, per_node, per_source),
                "node",
                split_axis=0,
                concat_axis=0,
                tiled=True,
            ),
            "local",
            split_axis=1,
            concat_axis=1,
            tiled=True,
        ),
    )
    slot_rows = rows_in.reshape(SLOTS, grad_out.shape[1])
    slot_gates = gates_in.reshape(SLOTS).astype(jnp.float32)[:, None]
    project = lax.dot_general(
        slot_rows, down_weight, (((1,), (1,)), ((), ())), preferred_element_type=jnp.float32
    )
    hidden_grad = (slot_gates * project).astype(jnp.bfloat16)
    wide_acts = hidden_act.astype(jnp.float32)
    partial_value = jnp.sum(wide_acts * project, axis=1)
    returned = lax.all_to_all(
        lax.all_to_all(
            partial_value.reshape(node_count, local_count, per_source),
            "node",
            split_axis=0,
            concat_axis=0,
            tiled=True,
        ),
        "local",
        split_axis=1,
        concat_axis=1,
        tiled=True,
    )
    scaled = (slot_gates * wide_acts).astype(jnp.bfloat16)
    weight_grad = lax.dot_general(
        scaled, slot_rows, (((0,), (0,)), ((), ())), preferred_element_type=jnp.float32
    )
    squares = jnp.sum(weight_grad * weight_grad)
    total_sq = lax.psum(squares, ("node", "local"))
    entry_count = node_count * local_count * down_weight.shape[0] * down_weight.shape[1]
    factor = clip_rms / jnp.sqrt(total_sq / jnp.float32(entry_count) + square_eps)
    clipped = (weight_grad * factor).astype(jnp.bfloat16)
    summed = returned.reshape(node_count, per_node, 2, per_source).sum(axis=2).reshape(routes_dev)
    router_grad = summed[target].reshape(TOK_DEV, TOP)
    return (clipped, hidden_grad, router_grad)


def solution(mesh):
    return jax.shard_map(
        per_device,
        mesh=mesh,
        in_specs=(
            P(("node", "local"), None),
            P(("node", "local"), None),
            P(("node", "local"), None),
            P(("node", "local"), None),
            P(None, ("node", "local")),
        ),
        out_specs=(
            P(("node", "local"), None),
            P(None, ("node", "local")),
            P(("node", "local"), None),
        ),
        check_vma=False,
    )
```

profile of v0, /device:TPU:1, one launch (start us, length us, event | category | flops | bytes accessed | tf_op | source)
XLA Modules:
  0.0 728.9 jit_solution(10702326467679548937)
XLA Ops:
  0.6 0.9 copy.71
  1.7 0.7 broadcast_multiply_fusion
  3.5 4.3 scatter_custom_fusion
  7.8 0.8 copy.69
  8.7 6.8 gather_fusion
  15.8 0.7 reshape.137
  16.5 6.5 all-to-all-start
  22.9 7.3 %gather_fusion.1 = bf16[1024,3584]{1,0:T(8,128)(2,1)} fusion(bf16[128,3584]{1,0:T(8,128)(2,1)S(1)} %copy-done, s32[1024]{0:T(1024)S(1)} %get-tuple-element.24), kind=kCustom, calls=%fused_computation.1 | custom fusion | bytes 14684160 | tf_op jit(solution)/shard_map/gather | solution.py:39
  30.3 9.4 %broadcast_in_dim.29 = bf16[8,16,2,8,3584]{4,3,2,1,0:T(8,128)(2,1)} broadcast(bf16[8,16,8,3584]{3,2,1,0:T(8,128)(2,1)} %bitcast.24), dimensions={0,1,3,4} | broadcast | bytes 22020096 | tf_op jit(solution)/shard_map/broadcast_in_dim | solution.py:18
  39.6 5.5 all-to-all-start.2
  45.3 0.7 copy.77
  46.0 160.5 %all-to-all-done.2 = bf16[8,32,8,3584]{3,2,1,0:T(8,128)(2,1)} async-done(((bf16[8,32,8,3584]{3,2,1,0:T(8,128)(2,1)}), bf16[8,32,8,3584]{3,2,1,0:T(8,128)(2,1)}, u32[]{:S(2)}, u32[]{:S(2)}) %all-to-all-start.2) | async-done | bytes 14680096 | tf_op jit(solution)/shard_map/all_to_all | solution.py:44
  206.5 10.4 %all-to-all-start.1 = ((bf16[8,32,8]{2,0,1:T(8,128)(2,1)}), bf16[8,32,8]{2,0,1:T(8,128)(2,1)S(1)}, u32[]{:S(2)}, u32[]{:S(2)}) async-start(bf16[8,32,8]{2,0,1:T(8,128)(2,1)} %copy.77), calls=%async_computation.1 | async-start | bytes 131072 | tf_op jit(solution)/shard_map/all_to_all | solution.py:56
  216.9 13.6 %copy.81 = bf16[8,32,8,3584]{3,2,0,1:T(8,128)(2,1)} copy(bf16[8,32,8,3584]{3,2,1,0:T(8,128)(2,1)} %all-to-all-done.2) | data formatting | bytes 29360128 | tf_op jit(solution)/shard_map/all_to_all | solution.py:44
  230.5 9.5 %all-to-all-start.3 = ((bf16[8,32,8,3584]{3,2,0,1:T(8,128)(2,1)}), bf16[8,32,8,3584]{3,2,0,1:T(8,128)(2,1)}, u32[]{:S(2)}, u32[]{:S(2)}) async-start(bf16[8,32,8,3584]{3,2,0,1:T(8,128)(2,1)} %copy.81), calls=%async_computation.3 | async-start | bytes 29360128 | tf_op jit(solution)/shard_map/all_to_all | solution.py:43
  239.9 2.4 copy.80
  242.7 329.0 %all-to-all-done.3 = bf16[8,32,8,3584]{3,2,0,1:T(8,128)(2,1)} async-done(((bf16[8,32,8,3584]{3,2,0,1:T(8,128)(2,1)}), bf16[8,32,8,3584]{3,2,0,1:T(8,128)(2,1)}, u32[]{:S(2)}, u32[]{:S(2)}) %all-to-all-start.3) | async-done | bytes 14680096 | tf_op jit(solution)/shard_map/all_to_all | solution.py:43
  571.7 8.4 %copy.82 = bf16[8,32,8,3584]{3,2,1,0:T(8,128)(2,1)S(1)} copy(bf16[8,32,8,3584]{3,2,0,1:T(8,128)(2,1)} %all-to-all-done.3) | data formatting | bytes 29360128 | tf_op jit(solution)/shard_map/all_to_all | solution.py:43
  580.1 8.1 %fusion.1 = (f32[2048]{0:T(1024)S(1)}, bf16[2048,512]{0,1:T(8,128)(2,1)S(1)}) fusion(bf16[2048,512]{0,1:T(8,128)(2,1)S(1)} %copy-done.4, f32[2048]{0:T(1024)S(1)} %reshape.100, bf16[2048,3584]{1,0:T(8,128)(2,1)S(1)} %bitcast.25, bf16[512,3584]{1,0:T(8,128)(2,1)S(1)} %copy-done.5), kind=kOutput, calls=%fused_computation.9 | convolution fusion | flops 7521433600 | bytes 22560768 | tf_op jit(solution)/shard_map/dot_general | solution.py:72
  588.4 0.7 reshape.139
  589.1 5.5 all-to-all-start.4
  594.6 14.2 %multiply_reduce_fusion = (f32[]{:T(128)}, f32[512,3584]{1,0:T(8,128)}) fusion(bf16[2048,3584]{1,0:T(8,128)(2,1)} %bitcast.26, bf16[2048,512]{0,1:T(8,128)(2,1)} %copy.80, f32[2048]{0:T(1024)S(1)} %reshape.100), kind=kOutput, calls=%fused_computation.5 | convolution fusion | flops 7523008512 | bytes 24125444 | tf_op jit(solution)/shard_map/dot_general | solution.py:92
  608.7 96.9 %psum.7 = f32[]{:T(128)} all-reduce(f32[]{:T(128)} %get-tuple-element.25), channel_id=1, replica_groups=mesh['node'=8,'local'=32] {'node','local'}, use_global_device_ids=true, to_apply=%region_5.6 | all-reduce | flops 1 | bytes 8 | tf_op jit(solution)/shard_map/psum | solution.py:96
  706.3 0.5 broadcast.94
  706.8 0.7 reduce
  707.5 0.7 copy.84
  708.3 5.9 all-to-all-start.5
  714.1 5.7 multiply_convert_fusion
  719.8 2.5 copy.86
  722.3 1.2 all-to-all-done.5
  723.6 4.5 gather_fusion.2
  728.2 0.7 copy.87
  (48 shorter events, 2.5 us)
Async XLA Ops:
  0.6 22.3 %copy-start = (bf16[128,3584]{1,0:T(8,128)(2,1)S(1)}, bf16[128,3584]{1,0:T(8,128)(2,1)}, u32[]{:S(2)}) copy-start(bf16[128,3584]{1,0:T(8,128)(2,1)} %param.5) | copy-start | bytes 2752516
  16.5 13.8 %all-to-all-start = ((bf16[8,2,128]{2,1,0:T(2,128)(2,1)}), bf16[8,2,128]{2,1,0:T(2,128)(2,1)S(1)}, u32[]{:S(2)}, u32[]{:S(2)}) async-start(bf16[8,2,128]{2,1,0:T(2,128)(2,1)} %reshape.137), calls=%async_computation | async-start | bytes 8192 | tf_op jit(solution)/shard_map/all_to_all | solution.py:57
  39.6 166.8 %all-to-all-start.2 = ((bf16[8,32,8,3584]{3,2,1,0:T(8,128)(2,1)}), bf16[8,32,8,3584]{3,2,1,0:T(8,128)(2,1)}, u32[]{:S(2)}, u32[]{:S(2)}) async-start(bf16[8,32,8,3584]{3,2,1,0:T(8,128)(2,1)} %bitcast.23), calls=%async_computation.2 | async-start | bytes 29360128 | tf_op jit(solution)/shard_map/all_to_all | solution.py:44
  206.5 24.0 %all-to-all-start.1 = ((bf16[8,32,8]{2,0,1:T(8,128)(2,1)}), bf16[8,32,8]{2,0,1:T(8,128)(2,1)S(1)}, u32[]{:S(2)}, u32[]{:S(2)}) async-start(bf16[8,32,8]{2,0,1:T(8,128)(2,1)} %copy.77), calls=%async_computation.1 | async-start | bytes 131072 | tf_op jit(solution)/shard_map/all_to_all | solution.py:56
  230.5 9.5 %copy-start.3 = (bf16[2048,512]{1,0:T(8,128)(2,1)S(1)}, bf16[2048,512]{1,0:T(8,128)(2,1)}, u32[]{:S(2)}) copy-start(bf16[2048,512]{1,0:T(8,128)(2,1)} %param.9) | copy-start | bytes 6291460
  230.5 341.2 %all-to-all-start.3 = ((bf16[8,32,8,3584]{3,2,0,1:T(8,128)(2,1)}), bf16[8,32,8,3584]{3,2,0,1:T(8,128)(2,1)}, u32[]{:S(2)}, u32[]{:S(2)}) async-start(bf16[8,32,8,3584]{3,2,0,1:T(8,128)(2,1)} %copy.81), calls=%async_computation.3 | async-start | bytes 29360128 | tf_op jit(solution)/shard_map/all_to_all | solution.py:43
  571.7 8.4 %copy-start.4 = (bf16[2048,512]{0,1:T(8,128)(2,1)S(1)}, bf16[2048,512]{0,1:T(8,128)(2,1)}, u32[]{:S(2)}) copy-start(bf16[2048,512]{0,1:T(8,128)(2,1)} %copy.80) | copy-start | bytes 6291460
  571.7 8.4 %copy-start.5 = (bf16[512,3584]{1,0:T(8,128)(2,1)S(1)}, bf16[512,3584]{1,0:T(8,128)(2,1)}, u32[]{:S(2)}) copy-start(bf16[512,3584]{1,0:T(8,128)(2,1)} %param.8) | copy-start | bytes 11010052
  580.1 8.1 %copy-start.2 = (bf16[8,32,8,3584]{3,2,1,0:T(8,128)(2,1)}, bf16[8,32,8,3584]{3,2,1,0:T(8,128)(2,1)S(1)}, u32[]{:S(2)}) copy-start(bf16[8,32,8,3584]{3,2,1,0:T(8,128)(2,1)S(1)} %copy.82) | copy-start | bytes 44040196
  589.1 117.2 %all-to-all-start.4 = ((f32[8,1,256]{2,1,0:T(1,128)}), f32[8,1,256]{2,1,0:T(1,128)S(1)}, u32[]{:S(2)}, u32[]{:S(2)}) async-start(f32[8,1,256]{2,1,0:T(1,128)} %reshape.139), calls=%async_computation.4 | async-start | bytes 16384 | tf_op jit(solution)/shard_map/all_to_all | solution.py:79
  708.3 15.2 %all-to-all-start.5 = ((f32[8,32,8]{2,0,1:T(8,128)}), f32[8,32,8]{2,0,1:T(8,128)S(1)}, u32[]{:S(2)}, u32[]{:S(2)}) async-start(f32[8,32,8]{2,0,1:T(8,128)} %copy.84), calls=%async_computation.5 | async-start | bytes 262144 | tf_op jit(solution)/shard_map/all_to_all | solution.py:78
  719.8 9.1 %copy-start.1 = (bf16[128,3584]{1,0:T(8,128)(2,1)S(1)}, bf16[128,3584]{1,0:T(8,128)(2,1)}, u32[]{:S(2)}) copy-start(bf16[128,3584]{1,0:T(8,128)(2,1)} %param.5) | copy-start | bytes 2752516
where the time goes:
time: 730 us; the launch traced here: 729 us
  waiting for transfers between devices  491 us (67%)
  blocking collectives  96.9 us (13%)
  local copies, waits for them, and re-layouts  66.7 us (9%)
  starting transfers between devices  43.1 us (6%)
  matrix products  22.3 us (3%)
  other arithmetic  7.68 us (1%)
    all_to_all x1, waiting for transfers between devices, per_device(): lax.all_to_all(lax.all_to_all(both_halves(send_rows, node_count, per_node...  329 us
    all_to_all x1, waiting for transfers between devices, per_device(): lax.all_to_all(both_halves(send_rows, node_count, per_node, per_source),...  160 us
    psum x1, blocking collectives, per_device(): total_sq = lax.psum(squares, ('node', 'local'))  96.9 us
  transfers between devices with their start and end apart: 6, of which 3 were waited for; matrix products, arithmetic and copies ran while one was open for 6% of the time, Pallas kernels for 0%

commit v1 on v0

v1 whole, which is shorter than its diff:
```python
import jax
import jax.numpy as jnp
from jax import lax
from jax.experimental import pallas as pl
from jax.experimental.pallas import tpu as pltpu
from jax.sharding import PartitionSpec as P

MESH = pl.DeviceIdType.MESH
F32 = jnp.float32
BF16 = jnp.bfloat16

D = 3584
FFH = 512
TOK = 128
SLOTS = 2048
ENTRIES = 469762048
CLIP = 0.25
EPS = 1e-06

CG = 1280
CA = D - CG
TW = D + CG
HALF = TW // 2
NB = 4
NZ = 8
CT = 256


def nt(a, b):
    return lax.dot_general(a, b, (((1,), (1,)), ((), ())), preferred_element_type=F32)


def step_z(z, k):
    return lax.rem(z + ((k + 1) // 2) * (1 - 2 * lax.rem(k, 2)) + NZ, NZ)


def kernel(
    tok_hbm, ids_ref, gate_ref, w_hbm, act_hbm,
    out_hbm, hg_hbm, router_ref,
    tx, rows, stage, wv, actv, hgv, wg, sel, meta, gvb, gvr, proj, sct, gate_s, rk_s,
    pv, a1, b1, a2, b2, a3, b3, a4, b4,
    in_sem, out_sem, meta_s, meta_r, zmeta_s, zmeta_r, pc_s, pc_r, zr_s, zr_r, sib_s, sib_r,
    fh_s, fh_r, fw_s, fw_r, gv_s, gv_r, e1_s, e1_r, e2_s, e2_r, e3_s, e3_r, e4_s, e4_r,
):
    node = lax.axis_index("node")
    local = lax.axis_index("local")
    y, c = node // 2, lax.rem(node, 2)
    z, x = local // 4, lax.rem(local, 4)
    xp = lax.rem(x, 2)
    pair = x // 2
    qx = lax.rem(xp + pair, 2)
    x_partner = x + 1 - 2 * xp
    me8 = pair * 4 + y

    def dev(xx, yy, zz, cc):
        return (2 * yy + cc, 4 * zz + xx)

    partner = dev(x_partner, y, z, c)
    sibling = dev(x, y, z, 1 - c)
    diagonal = dev(x_partner, y, z, 1 - c)

    def entry_x(p):
        return qx + p * (3 - 2 * qx)

    def remote(src, dst, ss, rs, to):
        return pltpu.make_async_remote_copy(
            src_ref=src, dst_ref=dst, send_sem=ss, recv_sem=rs, device_id=to, device_id_type=MESH
        )

    def landed(dst, rs):
        pltpu.make_async_copy(dst, dst, rs).wait()

    def zpeer(d):
        return dev(x, y, lax.rem(z + d + NZ, NZ), c)

    own_rows = pl.ds(pl.multiple_of(c * TOK, TOK), TOK)
    sib_rows = pl.ds(pl.multiple_of((1 - c) * TOK, TOK), TOK)
    tok_copy = pltpu.make_async_copy(tok_hbm, tx.at[z, own_rows, pl.ds(0, D)], in_sem.at[0])
    tok_copy.start()
    act_copy = pltpu.make_async_copy(act_hbm, actv, in_sem.at[1])
    w_copy = pltpu.make_async_copy(w_hbm, wv, in_sem.at[2])
    mine = xp * 2 + c
    meta[z, mine, 0:8, :] = ids_ref[...].astype(F32)
    meta[z, mine, 8:16, :] = gate_ref[...].astype(F32)

    barrier = pltpu.get_barrier_semaphore()

    def greet(to):
        pl.semaphore_signal(barrier, inc=1, device_id=to, device_id_type=MESH)

    for to in (partner, sibling, diagonal):
        greet(to)
    for d in range(1, NZ):
        greet(zpeer(d))
    for m in range(8):
        @pl.when(m != me8)
        def _(m=m):
            greet(dev(entry_x(m // 4), m % 4, z, c))
    pl.semaphore_wait(barrier, 3 + 7 + 7)

    others = ((partner, (1 - xp) * 2 + c), (sibling, xp * 2 + 1 - c), (diagonal, (1 - xp) * 2 + 1 - c))
    meta_copies = [
        remote(meta.at[z, mine], meta.at[z, mine], meta_s.at[j], meta_r.at[j], to)
        for j, (to, _) in enumerate(others)
    ]
    for cp in meta_copies:
        cp.start()
    tok_copy.wait()
    part_cols = (pl.ds(0, D), pl.ds(D, CG))
    pre = remote(
        tx.at[z, own_rows, pl.ds(CA, CG)], tx.at[z, own_rows, pl.ds(D, CG)], pc_s, pc_r, partner
    )
    pre.start()

    def zsend(zs, cols, ss, rs, d):
        return remote(tx.at[zs, own_rows, cols], tx.at[zs, own_rows, cols], ss, rs, zpeer(d))

    def sib_copy(zs, k, part):
        ref = tx.at[zs, own_rows, part_cols[part]]
        return remote(ref, ref, sib_s.at[k, part], sib_r.at[k, part], sibling)

    def own_send(part):
        zsend(z, part_cols[part], zr_s.at[0, part], zr_r.at[1, part], 1).start()
        zsend(z, part_cols[part], zr_s.at[7, part], zr_r.at[2, part], -1).start()
        sib_copy(z, 0, part).start()

    own_send(0)
    for j, (_, slot) in enumerate(others):
        landed(meta.at[z, slot], meta_r.at[j])
    zmeta = [
        remote(meta.at[z], meta.at[z], zmeta_s.at[d], zmeta_r.at[d], zpeer(d)) for d in range(1, NZ)
    ]
    for cp in zmeta:
        cp.start()
    act_copy.start()
    w_copy.start()
    pre.wait_recv()
    own_send(1)
    for d in range(1, NZ):
        landed(meta.at[lax.rem(z - d + NZ, NZ)], zmeta_r.at[d])

    row8 = lax.broadcasted_iota(jnp.int32, (8, TOK), 0)
    before = jnp.where(
        lax.broadcasted_iota(jnp.int32, (TOK, TOK), 0) < lax.broadcasted_iota(jnp.int32, (TOK, TOK), 1),
        1.0, 0.0,
    ).astype(BF16)
    expert8 = ((2 * lax.rem(row8, 4) + c) * 16 + 2 * z + row8 // 4).astype(F32)
    rank8 = row8.astype(F32)
    zero8 = jnp.zeros((8, TOK), F32)

    def build(k, carry):
        zs = step_z(z, k)
        for s in range(2):
            hits, gates = [], []
            for cs in range(2):
                one = meta[zs, lax.rem(xp + s, 2) * 2 + cs]
                hit_sum, gate_sum = zero8, zero8
                for kk in range(8):
                    hit = one[kk : kk + 1, :] == expert8
                    hit_sum += jnp.where(hit, 1.0, 0.0)
                    gate_sum += jnp.where(hit, one[8 + kk : 9 + kk, :], 0.0)
                hits.append(hit_sum)
                gates.append(gate_sum)
            hit16 = jnp.concatenate(hits, axis=0)
            rank = jnp.dot(hit16.astype(BF16), before, preferred_element_type=F32)
            rank = jnp.where(hit16 > 0.5, rank, -1.0)
            picks, gate_picks = [], []
            for m in range(8):
                for cs in range(2):
                    at = rank[cs * 8 + m : cs * 8 + m + 1, :] == rank8
                    pick = jnp.where(at, 1.0, 0.0)
                    gate_pick = jnp.where(at, gates[cs][m : m + 1, :], 0.0)
                    pair_of = (lambda t: [t, zero8]) if cs == 0 else (lambda t: [zero8, t])
                    picks.append(jnp.concatenate(pair_of(pick), axis=1))
                    gate_picks.append(jnp.concatenate(pair_of(gate_pick), axis=1))
            sel[k, s] = jnp.concatenate(picks, axis=0).astype(BF16)
            weighted = jnp.concatenate(gate_picks, axis=0).astype(BF16)
            gate_row = nt(jnp.ones((16, 2 * TOK), BF16), weighted)
            gvb[s, pl.ds(zs, 1), :] = gate_row[0:1]
        return carry

    lax.fori_loop(0, NZ, build, 0)

    def gv_copy(m):
        return remote(
            gvb, gvr.at[me8], gv_s.at[m], gv_r.at[me8], dev(entry_x(m // 4), m % 4, z, c)
        )

    gvr[me8] = gvb[...]
    for m in range(8):
        @pl.when(m != me8)
        def _(m=m):
            gv_copy(m).start()

    def z_arrive(k):
        zs = step_z(z, k)

        @pl.when(k <= 6)
        def _():
            for part in range(2):
                landed(tx.at[zs, own_rows, part_cols[part]], zr_r.at[k, part])

        @pl.when(k == 7)
        def _():
            for part in range(2):
                landed(tx.at[zs, own_rows, pl.ds(part * HALF, HALF)], zr_r.at[k, part])

        odd = lax.rem(k, 2) == 1

        @pl.when((k <= 4) & odd)
        def _():
            for part in range(2):
                zsend(zs, part_cols[part], zr_s.at[k, part], zr_r.at[k + 2, part], 1).start()

        @pl.when((k <= 4) & jnp.logical_not(odd))
        def _():
            for part in range(2):
                zsend(zs, part_cols[part], zr_s.at[k, part], zr_r.at[k + 2, part], -1).start()

        @pl.when(k == 5)
        def _():
            zsend(zs, pl.ds(0, HALF), zr_s.at[5, 0], zr_r.at[7, 0], 1).start()

        @pl.when(k == 6)
        def _():
            zsend(zs, pl.ds(HALF, HALF), zr_s.at[6, 0], zr_r.at[7, 1], -1).start()

        for part in range(2):
            sib_copy(zs, k, part).start()

    def row_of(q, i, ys):
        return pl.multiple_of(((q * 2 + i) * 4 + ys) * 16, 16)

    def fh_pair(k, zs, m, part):
        b = lax.rem(k, NB)
        src_rows = pl.ds(m * 16, 16)
        if part == 0:
            src = stage.at[b, src_rows, pl.ds(0, D)]
            dst = rows.at[zs, pl.ds(row_of(qx, pair, y), 16), pl.ds(0, D)]
        else:
            src = stage.at[b, src_rows, pl.ds(D, CG)]
            dst = rows.at[zs, pl.ds(row_of(1 - qx, pair, y), 16), pl.ds(CA, CG)]
        return src, dst

    def fh_copy(k, zs, m, part):
        src, dst = fh_pair(k, zs, m, part)
        return remote(
            src, dst, fh_s.at[lax.rem(k, NB), m * 2 + part], fh_r.at[k, me8 * 2 + part],
            dev(entry_x(m // 4), m % 4, z, c),
        )

    def fh_start(k, zs):
        for m in range(8):
            for part in range(2):
                @pl.when(m != me8)
                def _(m=m, part=part):
                    fh_copy(k, zs, m, part).start()

                @pl.when(m == me8)
                def _(m=m, part=part):
                    src, dst = fh_pair(k, zs, m, part)
                    pltpu.make_async_copy(src, dst, fh_r.at[k, me8 * 2 + part]).start()

    def fh_sent(k):
        for m in range(8):
            for part in range(2):
                @pl.when(m != me8)
                def _(m=m, part=part):
                    fh_copy(k, step_z(z, k), m, part).wait_send()

    def fh_landed(k, zs):
        for j in range(8):
            landed(
                rows.at[zs, pl.ds(row_of(qx, j // 4, j % 4), 16), pl.ds(0, D)], fh_r.at[k, j * 2]
            )
            landed(
                rows.at[zs, pl.ds(row_of(1 - qx, j // 4, j % 4), 16), pl.ds(CA, CG)],
                fh_r.at[k, j * 2 + 1],
            )

    def fw_copy(k, zs):
        ref = rows.at[zs, pl.ds(pl.multiple_of(qx * 128, 128), 128), pl.ds(0, CA)]
        return remote(ref, ref, fw_s.at[k], fw_r.at[k], partner)

    def gather(k, zs):
        b = lax.rem(k, NB)

        def tile(t, carry):
            s = jnp.where(t >= D // CT, 1, 0)
            cols = pl.ds(pl.multiple_of(t * CT, CT), CT)
            picked = jnp.dot(sel[k, s], tx[zs, :, cols], preferred_element_type=F32)
            stage[b, :, cols] = picked.astype(BF16)
            return carry

        lax.fori_loop(0, TW // CT, tile, 0)

    def chunk(k, zs):
        lane = lax.broadcasted_iota(jnp.int32, (256, 128), 1)
        row = lax.broadcasted_iota(jnp.int32, (256, 128), 0)
        mine16 = lane == me8 * 16 + lax.rem(row, 16)
        gate_rows = []
        for q in range(2):
            for j in range(8):
                one = gvr[j, lax.rem(qx + q, 2), pl.ds(zs, 1), :]
                gate_rows.append(jnp.broadcast_to(one, (16, 128)))
        picked = jnp.where(mine16, jnp.concatenate(gate_rows, axis=0), 0.0).astype(BF16)
        gate_s[...] = jnp.dot(picked, jnp.ones((128, 128), BF16), preferred_element_type=F32)

        def ktile(t, carry):
            cols = pl.ds(pl.multiple_of(t * 512, 512), 512)
            part = nt(rows[zs, :, cols], wv[:, cols])

            @pl.when(t == 0)
            def _():
                proj[...] = part

            @pl.when(t > 0)
            def _():
                proj[...] += part

            return carry

        lax.fori_loop(0, D // 512, ktile, 0)

        total = jnp.zeros((256, 128), F32)
        for ct in range(4):
            cols = pl.ds(ct * 128, 128)
            gate = gate_s[...]
            pr = proj[:, cols]
            blocks = [
                actv[pl.ds(pl.multiple_of(ns * 256 + zs * 32, 32), 32), cols].astype(F32) for ns in range(8)
            ]
            pieces = []
            for q in range(2):
                for i in range(2):
                    xs = q + i * (3 - 2 * q)
                    for ns in range(8):
                        pieces.append(blocks[ns][xs * 8 : xs * 8 + 8])
            act = jnp.concatenate(pieces, axis=0)
            total += act * pr
            hidden = gate * pr
            for ns in range(8):
                back = []
                for xs in range(4):
                    at = ((((xs % 2) + (xs // 2)) % 2 * 2 + xs // 2) * 8 + ns) * 8
                    back.append(hidden[at : at + 8])
                hgv[pl.ds(pl.multiple_of(ns * 256 + zs * 32, 32), 32), cols] = jnp.concatenate(
                    back, axis=0
                ).astype(BF16)
            sct[ct * 128 : ct * 128 + 128, :] = jnp.transpose(gate * act).astype(BF16)
        ones = jnp.ones((16, 128), BF16)
        hi = total.astype(BF16)
        rest = total - hi.astype(F32)
        mid = rest.astype(BF16)
        low = (rest - mid.astype(F32)).astype(BF16)
        sums = nt(ones, hi) + nt(ones, mid) + nt(ones, low)
        for q in range(2):
            pv[q, pl.ds(zs, 1), :] = sums[0:1, q * 128 : q * 128 + 128]

        def ctile(t, carry):
            cols = pl.ds(pl.multiple_of(t * CT, CT), CT)
            part = jnp.dot(sct[...], rows[zs, :, cols], preferred_element_type=F32)

            @pl.when(k == 0)
            def _():
                wg[:, cols] = part

            @pl.when(k > 0)
            def _():
                wg[:, cols] += part

            return carry

        lax.fori_loop(0, D // CT, ctile, 0)

    def body(k, carry):
        @pl.when(k <= 7)
        def _():
            zs = step_z(z, k)

            @pl.when(lax.rem(k, 2) == 1)
            def _():
                z_arrive(k)

                @pl.when(k < 7)
                def _():
                    z_arrive(k + 1)

            for part in range(2):
                landed(tx.at[zs, sib_rows, part_cols[part]], sib_r.at[k, part])

            @pl.when(k >= NB)
            def _():
                fh_sent(k - NB)

            gather(k, zs)
            fh_start(k, zs)

        @pl.when((k >= 1) & (k <= 8))
        def _():
            zs = step_z(z, k - 1)
            fh_landed(k - 1, zs)
            fw_copy(k - 1, zs).start()

        @pl.when(k == 2)
        def _():
            act_copy.wait()
            w_copy.wait()
            for j in range(8):
                @pl.when(j != me8)
                def _(j=j):
                    landed(gvr.at[j], gv_r.at[j])

        @pl.when(k >= 2)
        def _():
            zs = step_z(z, k - 2)
            other = pl.ds(pl.multiple_of((1 - qx) * 128, 128), 128)
            landed(rows.at[zs, other, pl.ds(0, CA)], fw_r.at[k - 2])
            chunk(k - 2, zs)

        return carry

    lax.fori_loop(0, NZ + 2, body, 0)

    hg_copy = pltpu.make_async_copy(hgv, hg_hbm, in_sem.at[1])
    hg_copy.start()

    def square(t, acc):
        w = wg[:, pl.ds(pl.multiple_of(t * CT, CT), CT)]
        s = jnp.sum((w * w).reshape(FFH // 8, 8, CT), axis=0)
        return acc + s[:, :128] + s[:, 128:]

    squares = lax.fori_loop(0, D // CT, square, jnp.zeros((8, 128), F32))
    a1[0] = pv[1 - qx]
    a1[1] = squares
    e1 = remote(a1, b1, e1_s, e1_r, partner)
    e1.start()
    own = meta[z, mine]
    ranks = []
    for m in range(8):
        for cc in range(2):
            expert = ((2 * (m % 4) + cc) * 16 + m // 4 + 2 * row8).astype(F32)
            hit_sum = zero8
            for kk in range(8):
                hit_sum += jnp.where(own[kk : kk + 1, :] == expert, 1.0, 0.0)
            ranks.append(hit_sum)
    hit128 = jnp.concatenate(ranks, axis=0)
    rank = jnp.dot(hit128.astype(BF16), before, preferred_element_type=F32)
    rk_s[...] = jnp.where(hit128 > 0.5, rank, -1.0)
    e1.wait_recv()
    back = pv[qx] + b1[0]
    squares = a1[1] + b1[1]
    for j in range(8):
        a2[j, 0] = jnp.concatenate(
            [back[:, j * 16 : j * 16 + 16], jnp.zeros((8, 112), F32)], axis=1
        )
        a2[j, 1] = squares

    def e2_copy(j):
        return remote(a2.at[j], b2.at[me8], e2_s.at[j], e2_r.at[me8], dev(entry_x(j // 4), j % 4, z, c))

    for j in range(8):
        @pl.when(j != me8)
        def _(j=j):
            e2_copy(j).start()
    b2[me8] = a2[me8]
    for j in range(8):
        @pl.when(j != me8)
        def _(j=j):
            landed(b2.at[j], e2_r.at[j])
    a3[0] = jnp.concatenate([b2[j, 0][:, 0:16] for j in range(8)], axis=1)
    total = b2[0, 1]
    for j in range(1, 8):
        total += b2[j, 1]
    a3[1] = total
    e3 = [remote(a3, b3.at[z], e3_s.at[d], e3_r.at[d], zpeer(d)) for d in range(1, NZ)]
    for cp in e3:
        cp.start()
    b3[z] = a3[...]
    for d in range(1, NZ):
        landed(b3.at[lax.rem(z - d + NZ, NZ)], e3_r.at[d])
    a4[0] = jnp.concatenate([b3[j, 0, pl.ds(z, 1), :] for j in range(NZ)], axis=0)
    total = b3[0, 1]
    for j in range(1, NZ):
        total += b3[j, 1]
    a4[1] = total
    e4 = remote(a4, b4, e4_s, e4_r, sibling)
    e4.start()

    for part in range(2):
        zsend(z, part_cols[part], zr_s.at[0, part], zr_r.at[1, part], 1).wait_send()
        zsend(z, part_cols[part], zr_s.at[7, part], zr_r.at[2, part], -1).wait_send()
        for k in range(1, 5):
            zsend(step_z(z, k), part_cols[part], zr_s.at[k, part], zr_r.at[k + 2, part], 1).wait_send()
        for k in range(NZ):
            sib_copy(step_z(z, k), k, part).wait_send()
    zsend(step_z(z, 5), pl.ds(0, HALF), zr_s.at[5, 0], zr_r.at[7, 0], 1).wait_send()
    zsend(step_z(z, 6), pl.ds(HALF, HALF), zr_s.at[6, 0], zr_r.at[7, 1], -1).wait_send()
    pre.wait_send()

    e4.wait_recv()
    total = jnp.sum(a4[1] + b4[1], keepdims=True)
    factor = CLIP / jnp.sqrt(total / ENTRIES + EPS)
    out_copies = []
    for j in range(4):
        block = pl.ds((j % 2) * TOK, TOK)

        def scale(t, carry, j=j, block=block):
            cols = pl.ds(pl.multiple_of(t * 512, 512), 512)
            tx[j // 2, block, cols] = (wg[j * TOK : j * TOK + TOK, cols] * factor).astype(BF16)
            return carry

        lax.fori_loop(0, D // 512, scale, 0)
        cp = pltpu.make_async_copy(
            tx.at[j // 2, block, pl.ds(0, D)], out_hbm.at[pl.ds(j * TOK, TOK)], out_sem.at[j]
        )
        cp.start()
        out_copies.append(cp)

    first = jnp.where(c == 0, a4[0], b4[0])
    second = jnp.where(c == 0, b4[0], a4[0])
    values = []
    for v in (first, second):
        shifted = jnp.concatenate([v[:, 8:], v[:, :8]], axis=1)
        values.append(jnp.where(c == 0, v, shifted))
    sums = [zero8] * 8
    for m in range(8):
        for cc in range(2):
            at = (m * 2 + cc) * 8
            rk = rk_s[at : at + 8, :]
            val = zero8
            for r in range(8):
                col = jnp.broadcast_to(values[cc][:, m * 16 + r : m * 16 + r + 1], (8, TOK))
                val += jnp.where(rk == float(r), col, 0.0)
            expert = ((2 * (m % 4) + cc) * 16 + m // 4 + 2 * row8).astype(F32)
            for kk in range(8):
                sums[kk] += jnp.where(own[kk : kk + 1, :] == expert, val, 0.0)
    router_ref[...] = jnp.concatenate([jnp.sum(s, axis=0, keepdims=True) for s in sums], axis=0)

    for cp in meta_copies + zmeta + [e1] + e3 + [e4]:
        cp.wait_send()
    for k in range(NZ - NB, NZ):
        fh_sent(k)
    for k in range(NZ):
        fw_copy(k, step_z(z, k)).wait_send()
    for m in range(8):
        @pl.when(m != me8)
        def _(m=m):
            gv_copy(m).wait_send()
            e2_copy(m).wait_send()
    hg_copy.wait()
    for cp in out_copies:
        cp.wait()


def per_device(grad_out, expert_ids, gate_probs, down_weight, hidden_act):
    anywhere = pl.BlockSpec(memory_space=pl.ANY)
    vmem = pl.BlockSpec(memory_space=pltpu.VMEM)
    dma = pltpu.SemaphoreType.DMA
    small = pltpu.VMEM((2, 8, 128), F32)
    clipped, hidden_grad, router = pl.pallas_call(
        kernel,
        out_shape=(
            jax.ShapeDtypeStruct((FFH, D), BF16),
            jax.ShapeDtypeStruct((SLOTS, FFH), BF16),
            jax.ShapeDtypeStruct((8, TOK), F32),
        ),
        in_specs=[anywhere, vmem, vmem, anywhere, anywhere],
        out_specs=(anywhere, anywhere, vmem),
        scratch_shapes=[
            pltpu.VMEM((NZ, 2 * TOK, TW), BF16),
            pltpu.VMEM((NZ, 256, D), BF16),
            pltpu.VMEM((NB, 128, TW), BF16),
            pltpu.VMEM((FFH, D), BF16),
            pltpu.VMEM((SLOTS, FFH), BF16),
            pltpu.VMEM((SLOTS, FFH), BF16),
            pltpu.VMEM((FFH, D), F32),
            pltpu.VMEM((NZ, 2, 128, 256), BF16),
            pltpu.VMEM((NZ, 4, 16, 128), F32),
            small,
            pltpu.VMEM((8, 2, 8, 128), F32),
            pltpu.VMEM((256, FFH), F32),
            pltpu.VMEM((FFH, 256), BF16),
            pltpu.VMEM((256, 128), F32),
            pltpu.VMEM((128, 128), F32),
            small,
            small,
            small,
            pltpu.VMEM((8, 2, 8, 128), F32),
            pltpu.VMEM((8, 2, 8, 128), F32),
            small,
            pltpu.VMEM((8, 2, 8, 128), F32),
            small,
            small,
            dma((3,)),
            dma((4,)),
            dma((3,)),
            dma((3,)),
            dma((NZ,)),
            dma((NZ,)),
            dma,
            dma,
            dma((NZ, 2)),
            dma((NZ, 2)),
            dma((NZ, 2)),
            dma((NZ, 2)),
            dma((NB, 16)),
            dma((NZ, 16)),
            dma((NZ,)),
            dma((NZ,)),
            dma((8,)),
            dma((8,)),
            dma,
            dma,
            dma((8,)),
            dma((8,)),
            dma((NZ,)),
            dma((NZ,)),
            dma,
            dma,
        ],
        compiler_params=pltpu.CompilerParams(
            collective_id=0, has_side_effects=True, vmem_limit_bytes=60 * 2**20
        ),
    )(grad_out, expert_ids.T, gate_probs.T, down_weight, hidden_act)
    return clipped, hidden_grad, router.T


def solution(mesh):
    both = ("node", "local")
    return jax.shard_map(
        per_device,
        mesh=mesh,
        in_specs=(P(both, None), P(both, None), P(both, None), P(both, None), P(None, both)),
        out_specs=(P(both, None), P(None, both), P(both, None)),
        check_vma=False,
    )
```

time: 730 us -> 225 us (0.31)
  waiting for transfers between devices: 491 us -> 0 us
  Pallas kernels: 0 us -> 218 us
  blocking collectives: 96.9 us -> 0 us
  local copies, waits for them, and re-layouts: 66.7 us -> 6.18 us
  starting transfers between devices: 43.1 us -> 0 us
  matrix products: 22.3 us -> 0 us
  other arithmetic: 7.68 us -> 0 us
    all_to_all x6 -> x0, waiting for transfers between devices: 491 us -> none  [the longest x1 329 us: per_device(): lax.all_to_all(lax.all_to_all(both_halves(send_rows, node_count, per_node...]
    pallas_call x0 -> x1, Pallas kernels: none -> 218 us  [per_device(): pl.pallas_call(kernel, out_shape=(jax.ShapeDtypeStruct((FFH, D), BF16), j...]
    psum x1 -> x0, blocking collectives: 96.9 us -> none  [per_device(): total_sq = lax.psum(squares, ('node', 'local'))]
    all_to_all x6 -> x0, starting transfers between devices: 43.1 us -> none  [the longest x1 10.4 us: per_device(): lax.all_to_all(lax.all_to_all(both_halves(gate_block, node_count, per_nod...]
    all_to_all x6 -> x0, local copies, waits for them, and re-layouts: 24.1 us -> none  [the longest x1 13.6 us: per_device(): lax.all_to_all(both_halves(send_rows, node_count, per_node, per_source),...]
    dot_general x2 -> x0, matrix products: 22.3 us -> none  [the longest x1 14.2 us: per_device(): lax.dot_general(scaled, slot_rows, (((0,), (0,)), ((), ())), preferred_el...]
    gather x3 -> x0, local copies, waits for them, and re-layouts: 18.7 us -> none  [the longest x1 7.32 us: per_device(): grad_out[sorted_routes // TOP]]
    broadcast_in_dim x4 -> x0, local copies, waits for them, and re-layouts: 9.49 us -> none  [both_halves(): jnp.broadcast_to(shaped, (node_count, per_node, 2, per_source) + trailing)]
  transfers between devices with their start and end apart: 6 -> 0, of which waited for: 3 -> 0; matrix products, arithmetic and copies ran while one was open for 6% -> 0% of each run, Pallas kernels for 0% -> 0%
where the time goes in v1:
time: 225 us
  Pallas kernels  218 us (97%)
  local copies, waits for them, and re-layouts  6.18 us (3%)
    pallas_call x1, Pallas kernels, per_device(): pl.pallas_call(kernel, out_shape=(jax.ShapeDtypeStruct((FFH, D), BF16), j...  218 us
    unnamed x7, local copies, waits for them, and re-layouts  6.18 us

profile of v1, /device:TPU:1, one launch (start us, length us, event | category | flops | bytes accessed | tf_op | source)
XLA Modules:
  0.0 224.7 jit_solution(6627604105821239359)
XLA Ops:
  0.6 217.9 %shard_map.76 = (bf16[512,3584]{1,0:T(8,128)(2,1)}, bf16[2048,512]{1,0:T(8,128)(2,1)}, f32[8,128]{1,0:T(8,128)}) custom-call(bf16[128,3584]{1,0:T(8,128)(2,1)} %tok_hbm.1, s32[8,128]{1,0:T(8,128)} %bitcast.4, bf16[8,128]{1,0:T(8,128)(2,1)} %bitcast.5, bf16[512,3584]{1,0:T(8,128)(2,1)} %w_hbm.1, bf16[2048,512]{1,0:T(8,128)(2,1)} %act_hbm.1), custom_call_target="tpu_custom_call" | custom-call | tf_op jit(solution)/shard_map/pallas_call | solution.py:561
  218.5 0.0 copy-start
  218.5 4.3 %copy.11 = bf16[512,3584]{1,0:T(8,128)(2,1)} copy(bf16[512,3584]{1,0:T(8,128)(2,1)} %get-tuple-element.12) | data formatting | bytes 7340032
  222.8 0.0 copy-done
  222.8 0.0 copy-start.1
  222.8 1.3 copy.12
  224.1 0.0 copy-done.1
  224.1 0.6 copy.13
Async XLA Ops:
  218.5 4.3 %copy-start = (bf16[2048,512]{1,0:T(8,128)(2,1)S(1)}, bf16[2048,512]{1,0:T(8,128)(2,1)}, u32[]{:S(2)}) copy-start(bf16[2048,512]{1,0:T(8,128)(2,1)} %get-tuple-element.13) | copy-start | bytes 6291460
  222.8 1.3 copy-start.1

commit v2 on v0

v2 whole, which is shorter than its diff:
```python
import jax
import jax.numpy as jnp
from jax import lax
from jax.experimental import pallas as pl
from jax.experimental.pallas import tpu as pltpu
from jax.sharding import PartitionSpec as P

MESH = pl.DeviceIdType.MESH
F32 = jnp.float32
BF16 = jnp.bfloat16

D = 3584
FFH = 512
TOK = 128
SLOTS = 2048
ENTRIES = 469762048
CLIP = 0.25
EPS = 1e-06

DH = D // 2
GH = 640
AH = DH - GH
TW = DH + GH
NB = 6
NZ = 8
STEPS = 2 * NZ


def nt(a, b):
    return lax.dot_general(a, b, (((1,), (1,)), ((), ())), preferred_element_type=F32)


def step_z(z, k):
    return lax.rem(z + ((k + 1) // 2) * (1 - 2 * lax.rem(k, 2)) + NZ, NZ)


def step_kh(j):
    g, u = (j + 2) // 4, lax.rem(j + 2, 4)
    mid = (g + 3) // 4 - g // 4
    h = mid * (u // 2) + (1 - mid) * lax.rem(u, 2)
    side = mid * lax.rem(u, 2)
    return mid * (2 * g - 1 + side) + (g // 4) * 7, h, side


def tiles(width):
    out, at = [], 0
    while at < width:
        size = min(256, width - at)
        out.append((at, size))
        at += size
    return out


def kernel(
    tok_hbm, ids_ref, gate_ref, w_hbm, act_hbm,
    wg_hbm, hg_hbm, router_ref, factor_ref,
    tx, rows, stage, wv, actv, hgv, wg, sel, meta, gvb, gvr, proj, sct, gate_s, rk_s,
    pv, a1, b1, a3, b3,
    in_sem, out_sem, meta_s, meta_r, zmeta_s, zmeta_r, pc_s, pc_r, zr_s, zr_r, sib_s, sib_r,
    fh_s, fh_r, fh_l, fw_s, fw_r, gv_s, gv_r, e1_s, e1_r, e3_s, e3_r,
):
    node = lax.axis_index("node")
    local = lax.axis_index("local")
    y, c = node // 2, lax.rem(node, 2)
    z, x = local // 4, lax.rem(local, 4)
    xp = lax.rem(x, 2)
    pair = x // 2
    qx = lax.rem(xp + pair, 2)
    x_partner = x + 1 - 2 * xp
    me8 = pair * 4 + y
    me16 = x * 4 + y

    def dev(xx, yy, zz, cc):
        return (2 * yy + cc, 4 * zz + xx)

    partner = dev(x_partner, y, z, c)
    sibling = dev(x, y, z, 1 - c)
    diagonal = dev(x_partner, y, z, 1 - c)

    def entry_x(p):
        return qx + p * (3 - 2 * qx)

    def remote(src, dst, ss, rs, to):
        return pltpu.make_async_remote_copy(
            src_ref=src, dst_ref=dst, send_sem=ss, recv_sem=rs, device_id=to, device_id_type=MESH
        )

    def landed(dst, rs):
        pltpu.make_async_copy(dst, dst, rs).wait()

    def zpeer(d, cc=None):
        return dev(x, y, lax.rem(z + d + NZ, NZ), c if cc is None else cc)

    own_rows = pl.ds(pl.multiple_of(c * TOK, TOK), TOK)
    sib_rows = pl.ds(pl.multiple_of((1 - c) * TOK, TOK), TOK)
    tok_copies = [
        pltpu.make_async_copy(
            tok_hbm.at[:, pl.ds(h * DH, DH)], tx.at[z, h, own_rows, pl.ds(0, DH)], in_sem.at[h]
        )
        for h in range(2)
    ]
    for cp in tok_copies:
        cp.start()
    act_copy = pltpu.make_async_copy(act_hbm, actv, in_sem.at[2])
    w_copy = pltpu.make_async_copy(w_hbm, wv, in_sem.at[3])
    act_copy.start()
    w_copy.start()
    mine = xp * 2 + c
    meta[z, mine] = jnp.concatenate(
        [ids_ref[...].astype(F32), gate_ref[...].astype(F32)], axis=0
    ).astype(BF16)

    barrier = pltpu.get_barrier_semaphore()

    def greet(to):
        pl.semaphore_signal(barrier, inc=1, device_id=to, device_id_type=MESH)

    for j in range(16):
        @pl.when(j != me16)
        def _(j=j):
            greet(dev(j // 4, j % 4, z, c))
    greet(sibling)
    greet(diagonal)
    for d in range(1, NZ):
        greet(zpeer(d))
        greet(zpeer(d, 1 - c))
    pl.semaphore_wait(barrier, 15 + 2 + 14)

    others = ((partner, (1 - xp) * 2 + c), (sibling, xp * 2 + 1 - c), (diagonal, (1 - xp) * 2 + 1 - c))
    meta_copies = [
        remote(meta.at[z, mine], meta.at[z, mine], meta_s.at[j], meta_r.at[j], to)
        for j, (to, _) in enumerate(others)
    ]
    for cp in meta_copies:
        cp.start()
    part_cols = (pl.ds(0, DH), pl.ds(DH, GH))
    pre = [
        remote(
            tx.at[z, h, own_rows, pl.ds(AH, GH)], tx.at[z, h, own_rows, pl.ds(DH, GH)],
            pc_s.at[h], pc_r.at[h], partner,
        )
        for h in range(2)
    ]

    def zsend(zs, h, part, ss, rs, d):
        ref = tx.at[zs, h, own_rows, part_cols[part]]
        return remote(ref, ref, ss, rs, zpeer(d))

    def sib_copy(zs, k, h, part):
        ref = tx.at[zs, h, own_rows, part_cols[part]]
        return remote(ref, ref, sib_s.at[k, h, part], sib_r.at[k, h, part], sibling)

    def own_sends(h, part):
        return (
            zsend(z, h, part, zr_s.at[0, h, part], zr_r.at[1, h, part], 1),
            zsend(z, h, part, zr_s.at[7, h, part], zr_r.at[2, h, part], -1),
            sib_copy(z, 0, h, part),
        )

    for h in range(2):
        tok_copies[h].wait()
        pre[h].start()
    for j, (_, slot) in enumerate(others):
        landed(meta.at[z, slot], meta_r.at[j])
    zmeta = [
        remote(meta.at[z], meta.at[z], zmeta_s.at[d], zmeta_r.at[d], zpeer(d)) for d in range(1, NZ)
    ]
    for cp in zmeta:
        cp.start()
    for cp in own_sends(0, 0):
        cp.start()

    row8 = lax.broadcasted_iota(jnp.int32, (8, TOK), 0)
    before = jnp.where(
        lax.broadcasted_iota(jnp.int32, (TOK, TOK), 0) < lax.broadcasted_iota(jnp.int32, (TOK, TOK), 1),
        1.0, 0.0,
    ).astype(BF16)
    expert8 = ((2 * lax.rem(row8, 4) + c) * 16 + 2 * z + row8 // 4).astype(F32)
    rank8 = row8.astype(F32)
    zero8 = jnp.zeros((8, TOK), F32)

    def build(k, carry):
        zs = step_z(z, k)
        for s in range(2):
            hits, gates = [], []
            for cs in range(2):
                one = meta[zs, lax.rem(xp + s, 2) * 2 + cs].astype(F32)
                hit_sum, gate_sum = zero8, zero8
                for kk in range(8):
                    hit = one[kk : kk + 1, :] == expert8
                    hit_sum += jnp.where(hit, 1.0, 0.0)
                    gate_sum += jnp.where(hit, one[8 + kk : 9 + kk, :], 0.0)
                hits.append(hit_sum)
                gates.append(gate_sum)
            hit16 = jnp.concatenate(hits, axis=0)
            rank = jnp.dot(hit16.astype(BF16), before, preferred_element_type=F32)
            rank = jnp.where(hit16 > 0.5, rank, -1.0)
            picks, gate_picks = [], []
            for m in range(8):
                for cs in range(2):
                    at = rank[cs * 8 + m : cs * 8 + m + 1, :] == rank8
                    pick = jnp.where(at, 1.0, 0.0)
                    gate_pick = jnp.where(at, gates[cs][m : m + 1, :], 0.0)
                    pair_of = (lambda t: [t, zero8]) if cs == 0 else (lambda t: [zero8, t])
                    picks.append(jnp.concatenate(pair_of(pick), axis=1))
                    gate_picks.append(jnp.concatenate(pair_of(gate_pick), axis=1))
            sel[k, s] = jnp.concatenate(picks, axis=0).astype(BF16)
            weighted = jnp.concatenate(gate_picks, axis=0).astype(BF16)
            gate_row = nt(jnp.ones((16, 2 * TOK), BF16), weighted)
            gvb[s, pl.ds(zs, 1), :] = gate_row[0:1]
        return carry

    def gv_copy(m):
        return remote(
            gvb, gvr.at[me8], gv_s.at[m], gv_r.at[me8], dev(entry_x(m // 4), m % 4, z, c)
        )

    build(0, 0)
    for h in range(2):
        if h:
            for cp in own_sends(h, 0):
                cp.start()
        pre[h].wait_recv()
        for cp in own_sends(h, 1):
            cp.start()
    wg[...] = jnp.zeros((FFH, D), F32)

    def z_arrive(k, h):
        zs = step_z(z, k)
        for part in range(2):
            landed(tx.at[zs, h, own_rows, part_cols[part]], zr_r.at[k, h, part])
        odd = lax.rem(k, 2)
        onward = (k <= 4) | ((k == 5) & (h == 0)) | ((k == 6) & (h == 1))
        to_k = k + 2 - k // 6

        @pl.when(onward & (odd == 1))
        def _():
            for part in range(2):
                zsend(zs, h, part, zr_s.at[k, h, part], zr_r.at[to_k, h, part], 1).start()

        @pl.when(onward & (odd == 0))
        def _():
            for part in range(2):
                zsend(zs, h, part, zr_s.at[k, h, part], zr_r.at[to_k, h, part], -1).start()

        for part in range(2):
            sib_copy(zs, k, h, part).start()

    def row_of(q, i, ys):
        return pl.multiple_of(((q * 2 + i) * 4 + ys) * 16, 16)

    def half(h, at, width):
        return pl.ds(pl.multiple_of(h * DH + at, 128), width)

    def fh_pair(j, m, part):
        k, h, _ = step_kh(j)
        zs = step_z(z, k)
        b = lax.rem(j, NB)
        src = stage.at[b, pl.ds(m * 16, 16), part_cols[part]]
        if part == 0:
            return src, rows.at[zs, pl.ds(row_of(qx, pair, y), 16), half(h, 0, DH)]
        return src, rows.at[zs, pl.ds(row_of(1 - qx, pair, y), 16), half(h, AH, GH)]

    def fh_start(j):
        b = lax.rem(j, NB)
        for part in range(2):
            for m in range(8):
                src, dst = fh_pair(j, m, part)

                @pl.when(m != me8)
                def _(m=m, src=src, dst=dst):
                    remote(src, dst, fh_s.at[b], fh_r.at[j], dev(entry_x(m // 4), m % 4, z, c)).start()

                @pl.when(m == me8)
                def _(src=src, dst=dst):
                    pltpu.make_async_copy(src, dst, fh_l.at[b]).start()

    def fh_sent(j):
        b = lax.rem(j, NB)
        landed(stage.at[b, pl.ds(0, 112)], fh_s.at[b])

    def fh_landed(j):
        b = lax.rem(j, NB)
        landed(stage.at[b, pl.ds(0, 112)], fh_r.at[j])
        landed(stage.at[b, pl.ds(0, 16)], fh_l.at[b])

    def fw_copy(j):
        k, h, _ = step_kh(j)
        ref = rows.at[step_z(z, k), pl.ds(pl.multiple_of(qx * 128, 128), 128), half(h, 0, AH)]
        return remote(ref, ref, fw_s.at[j], fw_r.at[j], partner)

    def gather(j):
        k, h, _ = step_kh(j)
        zs = step_z(z, k)
        b = lax.rem(j, NB)
        for s, (start, width) in enumerate(((0, DH), (DH, GH))):
            pick = sel[k, s]
            for at, size in tiles(width):
                cols = pl.ds(start + at, size)
                picked = jnp.dot(pick, tx[zs, h, :, cols], preferred_element_type=F32)
                stage[b, :, cols] = picked.astype(BF16)

    def acts(zs, cols):
        blocks = [
            actv[pl.ds(pl.multiple_of(ns * 256 + zs * 32, 32), 32), cols].astype(F32) for ns in range(8)
        ]
        pieces = []
        for q in range(2):
            for i in range(2):
                xs = q + i * (3 - 2 * q)
                for ns in range(8):
                    pieces.append(blocks[ns][xs * 8 : xs * 8 + 8])
        return jnp.concatenate(pieces, axis=0)

    def chunk(j):
        k, h, _ = step_kh(j)
        zs = step_z(z, k)
        slot = lax.rem(k, 2)

        @pl.when(h == 0)
        def _():
            lane = lax.broadcasted_iota(jnp.int32, (256, 128), 1)
            row = lax.broadcasted_iota(jnp.int32, (256, 128), 0)
            mine16 = lane == me8 * 16 + lax.rem(row, 16)
            gate_rows = []
            for q in range(2):
                for i in range(8):
                    one = gvr[i, lax.rem(qx + q, 2), pl.ds(zs, 1), :]
                    gate_rows.append(jnp.broadcast_to(one, (16, 128)))
            picked = jnp.where(mine16, jnp.concatenate(gate_rows, axis=0), 0.0).astype(BF16)
            gate = jnp.dot(picked, jnp.ones((128, 128), BF16), preferred_element_type=F32)
            gate_s[slot] = gate
            for ct in range(4):
                cols = pl.ds(ct * 128, 128)
                sct[slot, ct * 128 : ct * 128 + 128, :] = jnp.transpose(gate * acts(zs, cols)).astype(BF16)
            proj[slot] = jnp.zeros((256, FFH), F32)

        proj[slot] += nt(rows[zs, :, half(h, 0, DH)], wv[:, half(h, 0, DH)])

        @pl.when(h == 1)
        def _():
            total = jnp.zeros((256, 128), F32)
            for ct in range(4):
                cols = pl.ds(ct * 128, 128)
                pr = proj[slot, :, cols]
                total += acts(zs, cols) * pr
                hidden = gate_s[slot] * pr
                for ns in range(8):
                    back = []
                    for xs in range(4):
                        at = ((((xs % 2) + (xs // 2)) % 2 * 2 + xs // 2) * 8 + ns) * 8
                        back.append(hidden[at : at + 8])
                    hgv[pl.ds(pl.multiple_of(ns * 256 + zs * 32, 32), 32), cols] = jnp.concatenate(
                        back, axis=0
                    ).astype(BF16)
            ones = jnp.ones((16, 128), BF16)
            hi = total.astype(BF16)
            rest = total - hi.astype(F32)
            mid = rest.astype(BF16)
            low = (rest - mid.astype(F32)).astype(BF16)
            sums = nt(ones, hi) + nt(ones, mid) + nt(ones, low)
            for q in range(2):
                pv[q, pl.ds(zs, 1), :] = sums[0:1, q * 128 : q * 128 + 128]

        for at, size in tiles(DH):
            cols = half(h, at, size)
            wg[:, cols] += jnp.dot(sct[slot], rows[zs, :, cols], preferred_element_type=F32)

    def body(j, carry):
        @pl.when(j < STEPS)
        def _():
            k, h, side = step_kh(j)
            zs = step_z(z, k)

            @pl.when(j == 1)
            def _():
                for d in range(1, NZ):
                    landed(meta.at[lax.rem(z - d + NZ, NZ)], zmeta_r.at[d])
                lax.fori_loop(1, NZ, build, 0)
                gvr[me8] = gvb[...]
                for m in range(8):
                    @pl.when(m != me8)
                    def _(m=m):
                        gv_copy(m).start()

            @pl.when((k > 0) & (side == 0))
            def _():
                z_arrive(k, h)

                @pl.when(k < 7)
                def _():
                    z_arrive(k + 1, h)

            for part in range(2):
                landed(tx.at[zs, h, sib_rows, part_cols[part]], sib_r.at[k, h, part])

            @pl.when(j >= NB)
            def _():
                fh_sent(j - NB)

            gather(j)
            fh_start(j)

        @pl.when((j >= 1) & (j <= STEPS))
        def _():
            fh_landed(j - 1)
            fw_copy(j - 1).start()

        @pl.when(j == 2)
        def _():
            act_copy.wait()
            w_copy.wait()
            for i in range(8):
                @pl.when(i != me8)
                def _(i=i):
                    landed(gvr.at[i], gv_r.at[i])

        @pl.when(j >= 2)
        def _():
            k, h, _ = step_kh(j - 2)
            other = pl.ds(pl.multiple_of((1 - qx) * 128, 128), 128)
            landed(rows.at[step_z(z, k), other, half(h, 0, AH)], fw_r.at[j - 2])
            chunk(j - 2)

        return carry

    lax.fori_loop(0, STEPS + 2, body, 0)

    out_copies = [
        pltpu.make_async_copy(wg, wg_hbm, out_sem.at[0]),
        pltpu.make_async_copy(hgv, hg_hbm, out_sem.at[1]),
    ]
    for cp in out_copies:
        cp.start()

    squares = zero8
    for at, size in tiles(D):
        w = wg[:, at : at + size]
        s = jnp.sum((w * w).reshape(FFH // 8, 8, size), axis=0)
        squares += s[:, :128] + s[:, 128:]
    for j in range(16):
        xx, yy = j // 4, j % 4
        back = pv[(xx % 2 + xx // 2) % 2]
        lanes = (xx // 2 * 4 + yy) * 16
        a1[j, 0] = jnp.concatenate([back[:, lanes : lanes + 16], jnp.zeros((8, 112), F32)], axis=1)
        a1[j, 1] = squares

    def e1_copy(j):
        return remote(a1.at[j], b1.at[me16], e1_s.at[j], e1_r.at[me16], dev(j // 4, j % 4, z, c))

    for j in range(16):
        @pl.when(j != me16)
        def _(j=j):
            e1_copy(j).start()
    b1[me16] = a1[me16]

    own = meta[z, mine].astype(F32)
    ranks = []
    for m in range(8):
        for cc in range(2):
            expert = ((2 * (m % 4) + cc) * 16 + m // 4 + 2 * row8).astype(F32)
            hit_sum = zero8
            for kk in range(8):
                hit_sum += jnp.where(own[kk : kk + 1, :] == expert, 1.0, 0.0)
            ranks.append(hit_sum)
    hit128 = jnp.concatenate(ranks, axis=0)
    rank = jnp.dot(hit128.astype(BF16), before, preferred_element_type=F32)
    rk_s[...] = jnp.where(hit128 > 0.5, rank, -1.0)

    for j in range(16):
        @pl.when(j != me16)
        def _(j=j):
            landed(b1.at[j], e1_r.at[j])
    a3[0] = jnp.concatenate(
        [
            b1[2 * p * 4 + yy, 0][:, 0:16] + b1[(2 * p + 1) * 4 + yy, 0][:, 0:16]
            for p in range(2)
            for yy in range(4)
        ],
        axis=1,
    )
    total = b1[0, 1]
    for j in range(1, 16):
        total += b1[j, 1]
    a3[1] = total

    def e3_copy(d, cc):
        to_c = c if cc == 0 else 1 - c
        return remote(
            a3, b3.at[z, c], e3_s.at[d, cc], e3_r.at[d, cc], zpeer(d, to_c)
        )

    e3 = [e3_copy(d, cc) for d in range(NZ) for cc in range(2) if d or cc]
    for cp in e3:
        cp.start()
    b3[z, c] = a3[...]
    for d in range(NZ):
        for cc in range(2):
            if d or cc:
                from_c = c if cc == 0 else 1 - c
                landed(b3.at[lax.rem(z - d + NZ, NZ), from_c], e3_r.at[d, cc])
    total = zero8
    for zz in range(NZ):
        for cc in range(2):
            total += b3[zz, cc, 1]
    total = jnp.sum(total, keepdims=True)
    factor_ref[...] = jnp.broadcast_to(CLIP / jnp.sqrt(total / ENTRIES + EPS), (8, 128))

    values = []
    for cc in range(2):
        v = jnp.concatenate([b3[zz, cc, 0, pl.ds(z, 1), :] for zz in range(NZ)], axis=0)
        shifted = jnp.concatenate([v[:, 8:], v[:, :8]], axis=1)
        values.append(jnp.where(c == 0, v, shifted))
    sums = [zero8] * 8
    for m in range(8):
        for cc in range(2):
            at = (m * 2 + cc) * 8
            rk = rk_s[at : at + 8, :]
            val = zero8
            for r in range(8):
                col = jnp.broadcast_to(values[cc][:, m * 16 + r : m * 16 + r + 1], (8, TOK))
                val += jnp.where(rk == float(r), col, 0.0)
            expert = ((2 * (m % 4) + cc) * 16 + m // 4 + 2 * row8).astype(F32)
            for kk in range(8):
                sums[kk] += jnp.where(own[kk : kk + 1, :] == expert, val, 0.0)
    router_ref[...] = jnp.concatenate([jnp.sum(s, axis=0, keepdims=True) for s in sums], axis=0)

    for cp in meta_copies + zmeta + pre + e3:
        cp.wait_send()
    for h in range(2):
        for part in range(2):
            for cp in own_sends(h, part):
                cp.wait_send()
            for k in range(1, NZ):
                sib_copy(step_z(z, k), k, h, part).wait_send()
                if k <= 4 or (k == 5 and h == 0) or (k == 6 and h == 1):
                    zsend(
                        step_z(z, k), h, part, zr_s.at[k, h, part], zr_r.at[7, h, part], 1
                    ).wait_send()
    for j in range(STEPS - NB, STEPS):
        fh_sent(j)
    for j in range(STEPS):
        fw_copy(j).wait_send()
    for m in range(8):
        @pl.when(m != me8)
        def _(m=m):
            gv_copy(m).wait_send()
    for j in range(16):
        @pl.when(j != me16)
        def _(j=j):
            e1_copy(j).wait_send()
    for cp in out_copies:
        cp.wait()


BLOCKS = 8
BR = FFH // BLOCKS


def finish(wg_hbm, hg_hbm, router_in, factor_ref, out_hbm, hg_out, router_out, wide, narrow, sems, out_sems, hg_sem):
    hg_copy = pltpu.make_async_copy(hg_hbm, hg_out, hg_sem)
    loads = [
        pltpu.make_async_copy(wg_hbm.at[pl.ds(j * BR, BR)], wide.at[j], sems.at[j]) for j in range(BLOCKS)
    ]
    stores = [
        pltpu.make_async_copy(narrow.at[j], out_hbm.at[pl.ds(j * BR, BR)], out_sems.at[j]) for j in range(BLOCKS)
    ]
    for cp in loads:
        cp.start()
    hg_copy.start()
    router_out[...] = router_in[...]
    factor = factor_ref[0:1, 0:1]
    for j in range(BLOCKS):
        loads[j].wait()
        narrow[j] = (wide[j] * factor).astype(BF16)
        stores[j].start()
    for cp in stores:
        cp.wait()
    hg_copy.wait()


def per_device(grad_out, expert_ids, gate_probs, down_weight, hidden_act):
    anywhere = pl.BlockSpec(memory_space=pl.ANY)
    vmem = pl.BlockSpec(memory_space=pltpu.VMEM)
    dma = pltpu.SemaphoreType.DMA
    small = pltpu.VMEM((2, 8, 128), F32)
    weight_grad, hidden, router, factor = pl.pallas_call(
        kernel,
        out_shape=(
            jax.ShapeDtypeStruct((FFH, D), F32),
            jax.ShapeDtypeStruct((SLOTS, FFH), BF16),
            jax.ShapeDtypeStruct((8, TOK), F32),
            jax.ShapeDtypeStruct((8, 128), F32),
        ),
        in_specs=[anywhere, vmem, vmem, anywhere, anywhere],
        out_specs=(anywhere, anywhere, vmem, vmem),
        scratch_shapes=[
            pltpu.VMEM((NZ, 2, 2 * TOK, TW), BF16),
            pltpu.VMEM((NZ, 256, D), BF16),
            pltpu.VMEM((NB, 128, TW), BF16),
            pltpu.VMEM((FFH, D), BF16),
            pltpu.VMEM((SLOTS, FFH), BF16),
            pltpu.VMEM((SLOTS, FFH), BF16),
            pltpu.VMEM((FFH, D), F32),
            pltpu.VMEM((NZ, 2, 128, 256), BF16),
            pltpu.VMEM((NZ, 4, 16, 128), BF16),
            small,
            pltpu.VMEM((8, 2, 8, 128), F32),
            pltpu.VMEM((2, 256, FFH), F32),
            pltpu.VMEM((2, FFH, 256), BF16),
            pltpu.VMEM((2, 256, 128), F32),
            pltpu.VMEM((128, 128), F32),
            small,
            pltpu.VMEM((16, 2, 8, 128), F32),
            pltpu.VMEM((16, 2, 8, 128), F32),
            small,
            pltpu.VMEM((NZ, 2, 2, 8, 128), F32),
            dma((4,)),
            dma((2,)),
            dma((3,)),
            dma((3,)),
            dma((NZ,)),
            dma((NZ,)),
            dma((2,)),
            dma((2,)),
            dma((NZ, 2, 2)),
            dma((NZ, 2, 2)),
            dma((NZ, 2, 2)),
            dma((NZ, 2, 2)),
            dma((NB,)),
            dma((STEPS,)),
            dma((NB,)),
            dma((STEPS,)),
            dma((STEPS,)),
            dma((8,)),
            dma((8,)),
            dma((16,)),
            dma((16,)),
            dma((NZ, 2)),
            dma((NZ, 2)),
        ],
        compiler_params=pltpu.CompilerParams(
            collective_id=0, has_side_effects=True, vmem_limit_bytes=60 * 2**20
        ),
    )(grad_out, expert_ids.T, gate_probs.T, down_weight, hidden_act)
    clipped, hidden_grad, router = pl.pallas_call(
        finish,
        out_shape=(
            jax.ShapeDtypeStruct((FFH, D), BF16),
            jax.ShapeDtypeStruct((SLOTS, FFH), BF16),
            jax.ShapeDtypeStruct((8, TOK), F32),
        ),
        in_specs=[anywhere, anywhere, vmem, vmem],
        out_specs=(anywhere, anywhere, vmem),
        scratch_shapes=[
            pltpu.VMEM((BLOCKS, BR, D), F32),
            pltpu.VMEM((BLOCKS, BR, D), BF16),
            dma((BLOCKS,)),
            dma((BLOCKS,)),
            dma,
        ],
        compiler_params=pltpu.CompilerParams(vmem_limit_bytes=32 * 2**20),
    )(weight_grad, hidden, router, factor)
    return clipped, hidden_grad, router.T


def solution(mesh):
    both = ("node", "local")
    return jax.shard_map(
        per_device,
        mesh=mesh,
        in_specs=(P(both, None), P(both, None), P(both, None), P(both, None), P(None, both)),
        out_specs=(P(both, None), P(None, both), P(both, None)),
        check_vma=False,
    )
```

time: 730 us -> 180 us (0.25)
  waiting for transfers between devices: 491 us -> 0 us
  Pallas kernels: 0 us -> 173 us
  blocking collectives: 96.9 us -> 0 us
  local copies, waits for them, and re-layouts: 66.7 us -> 6.02 us
  starting transfers between devices: 43.1 us -> 0 us
  matrix products: 22.3 us -> 0 us
  other arithmetic: 7.68 us -> 0 us
    all_to_all x6 -> x0, waiting for transfers between devices: 491 us -> none  [the longest x1 329 us: per_device(): lax.all_to_all(lax.all_to_all(both_halves(send_rows, node_count, per_node...]
    pallas_call x0 -> x2, Pallas kernels: none -> 173 us  [the longest x1 168 us: per_device(): pl.pallas_call(kernel, out_shape=(jax.ShapeDtypeStruct((FFH, D), F32), ja...]
    psum x1 -> x0, blocking collectives: 96.9 us -> none  [per_device(): total_sq = lax.psum(squares, ('node', 'local'))]
    all_to_all x6 -> x0, starting transfers between devices: 43.1 us -> none  [the longest x1 10.4 us: per_device(): lax.all_to_all(lax.all_to_all(both_halves(gate_block, node_count, per_nod...]
    all_to_all x6 -> x0, local copies, waits for them, and re-layouts: 24.1 us -> none  [the longest x1 13.6 us: per_device(): lax.all_to_all(both_halves(send_rows, node_count, per_node, per_source),...]
    dot_general x2 -> x0, matrix products: 22.3 us -> none  [the longest x1 14.2 us: per_device(): lax.dot_general(scaled, slot_rows, (((0,), (0,)), ((), ())), preferred_el...]
    gather x3 -> x0, local copies, waits for them, and re-layouts: 18.7 us -> none  [the longest x1 7.32 us: per_device(): grad_out[sorted_routes // TOP]]
    broadcast_in_dim x4 -> x0, local copies, waits for them, and re-layouts: 9.49 us -> none  [both_halves(): jnp.broadcast_to(shaped, (node_count, per_node, 2, per_source) + trailing)]
  transfers between devices with their start and end apart: 6 -> 0, of which waited for: 3 -> 0; matrix products, arithmetic and copies ran while one was open for 6% -> 0% of each run, Pallas kernels for 0% -> 0%
where the time goes in v2:
time: 180 us
  Pallas kernels  173 us (96%)
  local copies, waits for them, and re-layouts  6.02 us (3%)
    pallas_call x1, Pallas kernels, per_device(): pl.pallas_call(kernel, out_shape=(jax.ShapeDtypeStruct((FFH, D), F32), ja...  168 us
    unnamed x8, local copies, waits for them, and re-layouts  6.02 us
    pallas_call x1, Pallas kernels, per_device(): pl.pallas_call(finish, out_shape=(jax.ShapeDtypeStruct((FFH, D), BF16), j...  5 us

profile of v2, /device:TPU:1, one launch (start us, length us, event | category | flops | bytes accessed | tf_op | source)
XLA Modules:
  0.0 179.8 jit_solution(333203360493374726)
XLA Ops:
  0.6 168.2 %shard_map.76 = (f32[512,3584]{1,0:T(8,128)}, bf16[2048,512]{1,0:T(8,128)(2,1)}, f32[8,128]{1,0:T(8,128)}, f32[8,128]{1,0:T(8,128)}) custom-call(bf16[128,3584]{1,0:T(8,128)(2,1)} %tok_hbm.1, s32[8,128]{1,0:T(8,128)} %bitcast.3, bf16[8,128]{1,0:T(8,128)(2,1)} %bitcast.4, bf16[512,3584]{1,0:T(8,128)(2,1)} %w_hbm.1, bf16[2048,512]{1,0:T(8,128)(2,1)} %act_hbm.1), custom_call_target="tpu_custom_call" | custom-call | tf_op jit(solution)/shard_map/pallas_call | solution.py:587
  168.8 0.0 copy-start
  168.8 3.1 %copy-done = f32[512,3584]{1,0:T(8,128)S(1)} copy-done((f32[512,3584]{1,0:T(8,128)S(1)}, f32[512,3584]{1,0:T(8,128)}, u32[]{:S(2)}) %copy-start) | copy-done | bytes 7340056
  171.9 0.0 copy-start.1
  171.9 1.6 copy-done.1
  173.5 0.0 copy-start.2
  173.5 0.7 copy-done.2
  174.2 0.0 copy-start.3
  174.2 0.7 copy-done.3
  174.8 5.0 %shard_map.77 = (bf16[512,3584]{1,0:T(8,128)(2,1)}, bf16[2048,512]{1,0:T(8,128)(2,1)}, f32[8,128]{1,0:T(8,128)}) custom-call(f32[512,3584]{1,0:T(8,128)S(1)} %copy-done, bf16[2048,512]{1,0:T(8,128)(2,1)S(1)} %copy-done.1, f32[8,128]{1,0:T(8,128)S(1)} %copy-done.2, f32[8,128]{1,0:T(8,128)S(1)} %copy-done.3), custom_call_target="tpu_custom_call" | custom-call | tf_op jit(solution)/shard_map/pallas_call | solution.py:646
Async XLA Ops:
  168.8 3.1 %copy-start = (f32[512,3584]{1,0:T(8,128)S(1)}, f32[512,3584]{1,0:T(8,128)}, u32[]{:S(2)}) copy-start(f32[512,3584]{1,0:T(8,128)} %get-tuple-element.10.wg_hbm) | copy-start | bytes 22020100
  171.9 1.6 copy-start.1
  173.5 0.7 copy-start.2
  174.2 0.7 copy-start.3

commit v3 on v2

--- a/solution.py
+++ b/solution.py
@@ -24,6 +24,8 @@
 NB = 6
 NZ = 8
 STEPS = 2 * NZ
+LF = 2
+LC = 4
 
 
 def nt(a, b):
@@ -54,9 +56,9 @@
 def kernel(
     tok_hbm, ids_ref, gate_ref, w_hbm, act_hbm,
     wg_hbm, hg_hbm, router_ref, factor_ref,
-    tx, rows, stage, wv, actv, hgv, wg, sel, meta, gvb, gvr, proj, sct, gate_s, rk_s,
+    tx, rows, stage, wv, actv, hgv, wg, sel, meta, metaz, gvb, gvr, proj, sct, gate_s, rk_s,
     pv, a1, b1, a3, b3,
-    in_sem, out_sem, meta_s, meta_r, zmeta_s, zmeta_r, pc_s, pc_r, zr_s, zr_r, sib_s, sib_r,
+    in_sem, out_sem, meta_s, meta_r, zmeta_s, zmeta_r, pack_s, pack_r, pc_s, pc_r, zr_s, zr_r, sib_s, sib_r,
     fh_s, fh_r, fh_l, fw_s, fw_r, gv_s, gv_r, e1_s, e1_r, e3_s, e3_r,
 ):
     node = lax.axis_index("node")
@@ -106,9 +108,9 @@
     act_copy.start()
     w_copy.start()
     mine = xp * 2 + c
-    meta[z, mine] = jnp.concatenate(
-        [ids_ref[...].astype(F32), gate_ref[...].astype(F32)], axis=0
-    ).astype(BF16)
+    routing = jnp.concatenate([ids_ref[...].astype(F32), gate_ref[...].astype(F32)], axis=0).astype(BF16)
+    meta[mine] = routing
+    metaz[mine, z] = routing
 
     barrier = pltpu.get_barrier_semaphore()
 
@@ -128,10 +130,18 @@
 
     others = ((partner, (1 - xp) * 2 + c), (sibling, xp * 2 + 1 - c), (diagonal, (1 - xp) * 2 + 1 - c))
     meta_copies = [
-        remote(meta.at[z, mine], meta.at[z, mine], meta_s.at[j], meta_r.at[j], to)
+        remote(meta.at[mine], meta.at[mine], meta_s.at[j], meta_r.at[j], to)
         for j, (to, _) in enumerate(others)
     ]
-    for cp in meta_copies:
+    zmeta = [
+        remote(metaz.at[mine, z], metaz.at[mine, z], zmeta_s.at[d], zmeta_r.at[d], zpeer(d))
+        for d in range(1, NZ)
+    ]
+    packs = [
+        remote(metaz.at[mine], metaz.at[mine], pack_s.at[j], pack_r.at[j], to)
+        for j, (to, _) in enumerate(others)
+    ]
+    for cp in meta_copies + zmeta:
         cp.start()
     part_cols = (pl.ds(0, DH), pl.ds(DH, GH))
     pre = [
@@ -150,25 +160,19 @@
         ref = tx.at[zs, h, own_rows, part_cols[part]]
         return remote(ref, ref, sib_s.at[k, h, part], sib_r.at[k, h, part], sibling)
 
-    def own_sends(h, part):
+    def own_zsends(h, part):
         return (
             zsend(z, h, part, zr_s.at[0, h, part], zr_r.at[1, h, part], 1),
             zsend(z, h, part, zr_s.at[7, h, part], zr_r.at[2, h, part], -1),
-            sib_copy(z, 0, h, part),
         )
 
     for h in range(2):
         tok_copies[h].wait()
         pre[h].start()
-    for j, (_, slot) in enumerate(others):
-        landed(meta.at[z, slot], meta_r.at[j])
-    zmeta = [
-        remote(meta.at[z], meta.at[z], zmeta_s.at[d], zmeta_r.at[d], zpeer(d)) for d in range(1, NZ)
-    ]
-    for cp in zmeta:
-        cp.start()
-    for cp in own_sends(0, 0):
-        cp.start()
+        sib_copy(z, 0, h, 0).start()
+        if h == 0:
+            for cp in own_zsends(0, 0):
+                cp.start()
 
     row8 = lax.broadcasted_iota(jnp.int32, (8, TOK), 0)
     before = jnp.where(
@@ -179,12 +183,12 @@
     rank8 = row8.astype(F32)
     zero8 = jnp.zeros((8, TOK), F32)
 
-    def build(k, carry):
+    def build_from(data, k):
         zs = step_z(z, k)
         for s in range(2):
             hits, gates = [], []
             for cs in range(2):
-                one = meta[zs, lax.rem(xp + s, 2) * 2 + cs].astype(F32)
+                one = data(lax.rem(xp + s, 2) * 2 + cs, zs).astype(F32)
                 hit_sum, gate_sum = zero8, zero8
                 for kk in range(8):
                     hit = one[kk : kk + 1, :] == expert8
@@ -208,22 +212,15 @@
             weighted = jnp.concatenate(gate_picks, axis=0).astype(BF16)
             gate_row = nt(jnp.ones((16, 2 * TOK), BF16), weighted)
             gvb[s, pl.ds(zs, 1), :] = gate_row[0:1]
+
+    def build(k, carry):
+        build_from(lambda who, zs: metaz[who, zs], k)
         return carry
 
     def gv_copy(m):
         return remote(
             gvb, gvr.at[me8], gv_s.at[m], gv_r.at[me8], dev(entry_x(m // 4), m % 4, z, c)
         )
-
-    build(0, 0)
-    for h in range(2):
-        if h:
-            for cp in own_sends(h, 0):
-                cp.start()
-        pre[h].wait_recv()
-        for cp in own_sends(h, 1):
-            cp.start()
-    wg[...] = jnp.zeros((FFH, D), F32)
 
     def z_arrive(k, h):
         zs = step_z(z, k)
@@ -256,23 +253,22 @@
         k, h, _ = step_kh(j)
         zs = step_z(z, k)
         b = lax.rem(j, NB)
-        src = stage.at[b, pl.ds(m * 16, 16), part_cols[part]]
+        src = stage.at[b, pl.ds(pl.multiple_of(m * 16, 16), 16), part_cols[part]]
         if part == 0:
             return src, rows.at[zs, pl.ds(row_of(qx, pair, y), 16), half(h, 0, DH)]
         return src, rows.at[zs, pl.ds(row_of(1 - qx, pair, y), 16), half(h, AH, GH)]
 
-    def fh_start(j):
+    def fh_start(j, parts=(0, 1)):
         b = lax.rem(j, NB)
-        for part in range(2):
-            for m in range(8):
+        for part in parts:
+            for far, dy in ((1, 2), (0, 2), (1, 1), (1, 3), (0, 1), (0, 3), (1, 0), (0, 0)):
+                yy = lax.rem(y + dy, 4)
+                m = (pair + far - 2 * far * pair) * 4 + yy
                 src, dst = fh_pair(j, m, part)
-
-                @pl.when(m != me8)
-                def _(m=m, src=src, dst=dst):
-                    remote(src, dst, fh_s.at[b], fh_r.at[j], dev(entry_x(m // 4), m % 4, z, c)).start()
-
-                @pl.when(m == me8)
-                def _(src=src, dst=dst):
+                if far or dy:
+                    xx = x + far * (3 - 2 * x)
+                    remote(src, dst, fh_s.at[b], fh_r.at[j], dev(xx, yy, z, c)).start()
+                else:
                     pltpu.make_async_copy(src, dst, fh_l.at[b]).start()
 
     def fh_sent(j):
@@ -289,11 +285,12 @@
         ref = rows.at[step_z(z, k), pl.ds(pl.multiple_of(qx * 128, 128), 128), half(h, 0, AH)]
         return remote(ref, ref, fw_s.at[j], fw_r.at[j], partner)
 
-    def gather(j):
+    def gather(j, parts=(0, 1)):
         k, h, _ = step_kh(j)
         zs = step_z(z, k)
         b = lax.rem(j, NB)
-        for s, (start, width) in enumerate(((0, DH), (DH, GH))):
+        for s in parts:
+            start, width = ((0, DH), (DH, GH))[s]
             pick = sel[k, s]
             for at, size in tiles(width):
                 cols = pl.ds(start + at, size)
@@ -372,17 +369,6 @@
             k, h, side = step_kh(j)
             zs = step_z(z, k)
 
-            @pl.when(j == 1)
-            def _():
-                for d in range(1, NZ):
-                    landed(meta.at[lax.rem(z - d + NZ, NZ)], zmeta_r.at[d])
-                lax.fori_loop(1, NZ, build, 0)
-                gvr[me8] = gvb[...]
-                for m in range(8):
-                    @pl.when(m != me8)
-                    def _(m=m):
-                        gv_copy(m).start()
-
             @pl.when((k > 0) & (side == 0))
             def _():
                 z_arrive(k, h)
@@ -401,12 +387,31 @@
             gather(j)
             fh_start(j)
 
-        @pl.when((j >= 1) & (j <= STEPS))
-        def _():
-            fh_landed(j - 1)
-            fw_copy(j - 1).start()
-
-        @pl.when(j == 2)
+        @pl.when(j == 1)
+        def _():
+            for d in range(1, NZ):
+                landed(metaz.at[mine, lax.rem(z - d + NZ, NZ)], zmeta_r.at[d])
+            for cp in packs:
+                cp.start()
+
+        @pl.when((j >= LF) & (j < STEPS + LF))
+        def _():
+            fh_landed(j - LF)
+            fw_copy(j - LF).start()
+
+        @pl.when(j == 1)
+        def _():
+            for i, (_, slot) in enumerate(others):
+                landed(metaz.at[slot], pack_r.at[i])
+            lax.fori_loop(1, NZ, build, 0)
+            gvr[me8] = gvb[...]
+            for m in range(8):
+                @pl.when(m != me8)
+                def _(m=m):
+                    gv_copy(m).start()
+            wg[...] = jnp.zeros((FFH, D), F32)
+
+        @pl.when(j == LC)
         def _():
             act_copy.wait()
             w_copy.wait()
@@ -415,16 +420,34 @@
                 def _(i=i):
                     landed(gvr.at[i], gv_r.at[i])
 
-        @pl.when(j >= 2)
-        def _():
-            k, h, _ = step_kh(j - 2)
+        @pl.when(j >= LC)
+        def _():
+            k, h, _ = step_kh(j - LC)
             other = pl.ds(pl.multiple_of((1 - qx) * 128, 128), 128)
-            landed(rows.at[step_z(z, k), other, half(h, 0, AH)], fw_r.at[j - 2])
-            chunk(j - 2)
+            landed(rows.at[step_z(z, k), other, half(h, 0, AH)], fw_r.at[j - LC])
+            chunk(j - LC)
 
         return carry
 
-    lax.fori_loop(0, STEPS + 2, body, 0)
+    for j, (_, slot) in enumerate(others):
+        landed(meta.at[slot], meta_r.at[j])
+    build_from(lambda who, zs: meta[who], 0)
+    for part in range(2):
+        if part == 1:
+            pre[0].wait_recv()
+            for cp in own_zsends(0, 1):
+                cp.start()
+            sib_copy(z, 0, 0, 1).start()
+            for cp in own_zsends(1, 0):
+                cp.start()
+        landed(tx.at[z, 0, sib_rows, part_cols[part]], sib_r.at[0, 0, part])
+        gather(0, (part,))
+        fh_start(0, (part,))
+    pre[1].wait_recv()
+    for cp in own_zsends(1, 1):
+        cp.start()
+    sib_copy(z, 0, 1, 1).start()
+    lax.fori_loop(1, STEPS + LC, body, 0)
 
     out_copies = [
         pltpu.make_async_copy(wg, wg_hbm, out_sem.at[0]),
@@ -454,7 +477,7 @@
             e1_copy(j).start()
     b1[me16] = a1[me16]
 
-    own = meta[z, mine].astype(F32)
+    own = meta[mine].astype(F32)
     ranks = []
     for m in range(8):
         for cc in range(2):
@@ -525,15 +548,15 @@
                 sums[kk] += jnp.where(own[kk : kk + 1, :] == expert, val, 0.0)
     router_ref[...] = jnp.concatenate([jnp.sum(s, axis=0, keepdims=True) for s in sums], axis=0)
 
-    for cp in meta_copies + zmeta + pre + e3:
+    for cp in meta_copies + zmeta + packs + pre + e3:
         cp.wait_send()
     for h in range(2):
         for part in range(2):
-            for cp in own_sends(h, part):
+            for cp in own_zsends(h, part):
                 cp.wait_send()
-            for k in range(1, NZ):
+            for k in range(NZ):
                 sib_copy(step_z(z, k), k, h, part).wait_send()
-                if k <= 4 or (k == 5 and h == 0) or (k == 6 and h == 1):
+                if 1 <= k <= 4 or (k == 5 and h == 0) or (k == 6 and h == 1):
                     zsend(
                         step_z(z, k), h, part, zr_s.at[k, h, part], zr_r.at[7, h, part], 1
                     ).wait_send()
@@ -557,23 +580,28 @@
 BR = FFH // BLOCKS
 
 
-def finish(wg_hbm, hg_hbm, router_in, factor_ref, out_hbm, hg_out, router_out, wide, narrow, sems, out_sems, hg_sem):
-    hg_copy = pltpu.make_async_copy(hg_hbm, hg_out, hg_sem)
+def finish(wg_hbm, hg_hbm, router_in, factor_ref, out_hbm, hg_out, router_out, wide, narrow, hidden, sems, out_sems, hg_sem):
+    hg_in = pltpu.make_async_copy(hg_hbm, hidden, hg_sem.at[0])
+    hg_copy = pltpu.make_async_copy(hidden, hg_out, hg_sem.at[1])
     loads = [
         pltpu.make_async_copy(wg_hbm.at[pl.ds(j * BR, BR)], wide.at[j], sems.at[j]) for j in range(BLOCKS)
     ]
     stores = [
         pltpu.make_async_copy(narrow.at[j], out_hbm.at[pl.ds(j * BR, BR)], out_sems.at[j]) for j in range(BLOCKS)
     ]
-    for cp in loads:
+    loads[0].start()
+    hg_in.start()
+    for cp in loads[1:]:
         cp.start()
-    hg_copy.start()
     router_out[...] = router_in[...]
     factor = factor_ref[0:1, 0:1]
     for j in range(BLOCKS):
         loads[j].wait()
         narrow[j] = (wide[j] * factor).astype(BF16)
         stores[j].start()
+        if j == 0:
+            hg_in.wait()
+            hg_copy.start()
     for cp in stores:
         cp.wait()
     hg_copy.wait()
@@ -603,7 +631,8 @@
             pltpu.VMEM((SLOTS, FFH), BF16),
             pltpu.VMEM((FFH, D), F32),
             pltpu.VMEM((NZ, 2, 128, 256), BF16),
-            pltpu.VMEM((NZ, 4, 16, 128), BF16),
+            pltpu.VMEM((4, 16, 128), BF16),
+            pltpu.VMEM((4, NZ, 16, 128), BF16),
             small,
             pltpu.VMEM((8, 2, 8, 128), F32),
             pltpu.VMEM((2, 256, FFH), F32),
@@ -621,6 +650,8 @@
             dma((3,)),
             dma((NZ,)),
             dma((NZ,)),
+            dma((3,)),
+            dma((3,)),
             dma((2,)),
             dma((2,)),
             dma((NZ, 2, 2)),
@@ -655,11 +686,12 @@
         scratch_shapes=[
             pltpu.VMEM((BLOCKS, BR, D), F32),
             pltpu.VMEM((BLOCKS, BR, D), BF16),
+            pltpu.VMEM((SLOTS, FFH), BF16),
             dma((BLOCKS,)),
             dma((BLOCKS,)),
-            dma,
+            dma((2,)),
         ],
-        compiler_params=pltpu.CompilerParams(vmem_limit_bytes=32 * 2**20),
+        compiler_params=pltpu.CompilerParams(vmem_limit_bytes=60 * 2**20),
     )(weight_grad, hidden, router, factor)
     return clipped, hidden_grad, router.T
 

time: 180 us -> 163 us (0.906)
  Pallas kernels: 173 us -> 162 us
  local copies, waits for them, and re-layouts: 6.02 us -> 0 us
    pallas_call x1, Pallas kernels: 168 us -> 155 us  [per_device(): pl.pallas_call(kernel, out_shape=(jax.ShapeDtypeStruct((FFH, D), F32), ja...]
    unnamed x8 -> x0, local copies, waits for them, and re-layouts: 6.02 us -> none
    pallas_call x1, Pallas kernels: 5 us -> 7.47 us  [per_device(): pl.pallas_call(finish, out_shape=(jax.ShapeDtypeStruct((FFH, D), BF16), j...]
where the time goes in v3:
time: 163 us
  Pallas kernels  162 us (99%)
    pallas_call x1, Pallas kernels, per_device(): pl.pallas_call(kernel, out_shape=(jax.ShapeDtypeStruct((FFH, D), F32), ja...  155 us
    pallas_call x1, Pallas kernels, per_device(): pl.pallas_call(finish, out_shape=(jax.ShapeDtypeStruct((FFH, D), BF16), j...  7.47 us

profile of v3, /device:TPU:1, one launch (start us, length us, event | category | flops | bytes accessed | tf_op | source)
XLA Modules:
  0.0 163.0 jit_solution(2032313039071305681)
XLA Ops:
  0.6 154.9 %shard_map.76 = (f32[512,3584]{1,0:T(8,128)}, bf16[2048,512]{1,0:T(8,128)(2,1)}, f32[8,128]{1,0:T(8,128)}, f32[8,128]{1,0:T(8,128)}) custom-call(bf16[128,3584]{1,0:T(8,128)(2,1)} %tok_hbm.1, s32[8,128]{1,0:T(8,128)} %bitcast.3, bf16[8,128]{1,0:T(8,128)(2,1)} %bitcast.4, bf16[512,3584]{1,0:T(8,128)(2,1)} %w_hbm.1, bf16[2048,512]{1,0:T(8,128)(2,1)} %act_hbm.1), custom_call_target="tpu_custom_call" | custom-call | tf_op jit(solution)/shard_map/pallas_call | solution.py:615
  155.6 7.5 %shard_map.77 = (bf16[512,3584]{1,0:T(8,128)(2,1)}, bf16[2048,512]{1,0:T(8,128)(2,1)}, f32[8,128]{1,0:T(8,128)}) custom-call(f32[512,3584]{1,0:T(8,128)} %get-tuple-element.10.wg_hbm, bf16[2048,512]{1,0:T(8,128)(2,1)} %get-tuple-element.11.hg_hbm, f32[8,128]{1,0:T(8,128)} %get-tuple-element.12.router_in, f32[8,128]{1,0:T(8,128)} %get-tuple-element.13.factor_ref), custom_call_target="tpu_custom_call" | custom-call | tf_op jit(solution)/shard_map/pallas_call | solution.py:677

commit v4 on v3

--- a/solution.py
+++ b/solution.py
@@ -24,6 +24,8 @@
 NB = 6
 NZ = 8
 STEPS = 2 * NZ
+PIECES = ((0, AH), (AH, GH), (DH, GH))
+WAITS = ((0, AH), (AH, TW - AH))
 LF = 2
 LC = 4
 
@@ -56,7 +58,7 @@
 def kernel(
     tok_hbm, ids_ref, gate_ref, w_hbm, act_hbm,
     wg_hbm, hg_hbm, router_ref, factor_ref,
-    tx, rows, stage, wv, actv, hgv, wg, sel, meta, metaz, gvb, gvr, proj, sct, gate_s, rk_s,
+    tx, rows, stage, wv, actv, hgv, wg, sel, meta, metaz, gvb, gvr, proj, sct, gate_s, rk_s, sq_s,
     pv, a1, b1, a3, b3,
     in_sem, out_sem, meta_s, meta_r, zmeta_s, zmeta_r, pack_s, pack_r, pc_s, pc_r, zr_s, zr_r, sib_s, sib_r,
     fh_s, fh_r, fh_l, fw_s, fw_r, gv_s, gv_r, e1_s, e1_r, e3_s, e3_r,
@@ -253,12 +255,12 @@
         k, h, _ = step_kh(j)
         zs = step_z(z, k)
         b = lax.rem(j, NB)
-        src = stage.at[b, pl.ds(pl.multiple_of(m * 16, 16), 16), part_cols[part]]
-        if part == 0:
-            return src, rows.at[zs, pl.ds(row_of(qx, pair, y), 16), half(h, 0, DH)]
-        return src, rows.at[zs, pl.ds(row_of(1 - qx, pair, y), 16), half(h, AH, GH)]
-
-    def fh_start(j, parts=(0, 1)):
+        start, width = PIECES[part]
+        src = stage.at[b, pl.ds(pl.multiple_of(m * 16, 16), 16), pl.ds(start, width)]
+        source = 1 - qx if part == 2 else qx
+        return src, rows.at[zs, pl.ds(row_of(source, pair, y), 16), half(h, min(start, AH), width)]
+
+    def fh_start(j, parts):
         b = lax.rem(j, NB)
         for part in parts:
             for far, dy in ((1, 2), (0, 2), (1, 1), (1, 3), (0, 1), (0, 3), (1, 0), (0, 0)):
@@ -267,25 +269,26 @@
                 src, dst = fh_pair(j, m, part)
                 if far or dy:
                     xx = x + far * (3 - 2 * x)
-                    remote(src, dst, fh_s.at[b], fh_r.at[j], dev(xx, yy, z, c)).start()
+                    remote(src, dst, fh_s.at[b], fh_r.at[j, min(part, 1)], dev(xx, yy, z, c)).start()
                 else:
-                    pltpu.make_async_copy(src, dst, fh_l.at[b]).start()
+                    pltpu.make_async_copy(src, dst, fh_l.at[b, min(part, 1)]).start()
 
     def fh_sent(j):
         b = lax.rem(j, NB)
         landed(stage.at[b, pl.ds(0, 112)], fh_s.at[b])
 
-    def fh_landed(j):
+    def fh_landed(j, group):
         b = lax.rem(j, NB)
-        landed(stage.at[b, pl.ds(0, 112)], fh_r.at[j])
-        landed(stage.at[b, pl.ds(0, 16)], fh_l.at[b])
+        cols = pl.ds(*WAITS[group])
+        landed(stage.at[b, pl.ds(0, 112), cols], fh_r.at[j, group])
+        landed(stage.at[b, pl.ds(0, 16), cols], fh_l.at[b, group])
 
     def fw_copy(j):
         k, h, _ = step_kh(j)
         ref = rows.at[step_z(z, k), pl.ds(pl.multiple_of(qx * 128, 128), 128), half(h, 0, AH)]
         return remote(ref, ref, fw_s.at[j], fw_r.at[j], partner)
 
-    def gather(j, parts=(0, 1)):
+    def gather(j, parts):
         k, h, _ = step_kh(j)
         zs = step_z(z, k)
         b = lax.rem(j, NB)
@@ -363,6 +366,18 @@
             cols = half(h, at, size)
             wg[:, cols] += jnp.dot(sct[slot], rows[zs, :, cols], preferred_element_type=F32)
 
+    def square(at):
+        acc = zero8
+        for start, size in tiles(DH):
+            w = wg[:, at + start : at + start + size]
+            s = jnp.sum((w * w).reshape(FFH // 8, 8, size), axis=0)
+            acc += s[:, :128] + s[:, 128:]
+        return acc
+
+    def wg_copy(h):
+        cols = pl.ds(h * DH, DH)
+        return pltpu.make_async_copy(wg.at[:, cols], wg_hbm.at[:, cols], out_sem.at[h])
+
     def body(j, carry):
         @pl.when(j < STEPS)
         def _():
@@ -384,8 +399,10 @@
             def _():
                 fh_sent(j - NB)
 
-            gather(j)
-            fh_start(j)
+            gather(j, (0,))
+            fh_start(j, (0, 1))
+            gather(j, (1,))
+            fh_start(j, (2,))
 
         @pl.when(j == 1)
         def _():
@@ -396,7 +413,7 @@
 
         @pl.when((j >= LF) & (j < STEPS + LF))
         def _():
-            fh_landed(j - LF)
+            fh_landed(j - LF, 0)
             fw_copy(j - LF).start()
 
         @pl.when(j == 1)
@@ -425,7 +442,13 @@
             k, h, _ = step_kh(j - LC)
             other = pl.ds(pl.multiple_of((1 - qx) * 128, 128), 128)
             landed(rows.at[step_z(z, k), other, half(h, 0, AH)], fw_r.at[j - LC])
+            fh_landed(j - LC, 1)
             chunk(j - LC)
+
+        @pl.when(j == STEPS + LC - 2)
+        def _():
+            sq_s[...] = square(0)
+            wg_copy(0).start()
 
         return carry
 
@@ -442,25 +465,18 @@
                 cp.start()
         landed(tx.at[z, 0, sib_rows, part_cols[part]], sib_r.at[0, 0, part])
         gather(0, (part,))
-        fh_start(0, (part,))
+        fh_start(0, (0, 1) if part == 0 else (2,))
     pre[1].wait_recv()
     for cp in own_zsends(1, 1):
         cp.start()
     sib_copy(z, 0, 1, 1).start()
     lax.fori_loop(1, STEPS + LC, body, 0)
 
-    out_copies = [
-        pltpu.make_async_copy(wg, wg_hbm, out_sem.at[0]),
-        pltpu.make_async_copy(hgv, hg_hbm, out_sem.at[1]),
-    ]
-    for cp in out_copies:
-        cp.start()
-
-    squares = zero8
-    for at, size in tiles(D):
-        w = wg[:, at : at + size]
-        s = jnp.sum((w * w).reshape(FFH // 8, 8, size), axis=0)
-        squares += s[:, :128] + s[:, 128:]
+    hg_copy = pltpu.make_async_copy(hgv, hg_hbm, out_sem.at[2])
+    wg_copy(1).start()
+    hg_copy.start()
+
+    squares = sq_s[...] + square(DH)
     for j in range(16):
         xx, yy = j // 4, j % 4
         back = pv[(xx % 2 + xx // 2) % 2]
@@ -572,8 +588,9 @@
         @pl.when(j != me16)
         def _(j=j):
             e1_copy(j).wait_send()
-    for cp in out_copies:
-        cp.wait()
+    hg_copy.wait()
+    for h in range(2):
+        wg_copy(h).wait()
 
 
 BLOCKS = 8
@@ -639,13 +656,14 @@
             pltpu.VMEM((2, FFH, 256), BF16),
             pltpu.VMEM((2, 256, 128), F32),
             pltpu.VMEM((128, 128), F32),
+            pltpu.VMEM((8, 128), F32),
             small,
             pltpu.VMEM((16, 2, 8, 128), F32),
             pltpu.VMEM((16, 2, 8, 128), F32),
             small,
             pltpu.VMEM((NZ, 2, 2, 8, 128), F32),
             dma((4,)),
-            dma((2,)),
+            dma((3,)),
             dma((3,)),
             dma((3,)),
             dma((NZ,)),
@@ -659,8 +677,8 @@
             dma((NZ, 2, 2)),
             dma((NZ, 2, 2)),
             dma((NB,)),
-            dma((STEPS,)),
-            dma((NB,)),
+            dma((STEPS, 2)),
+            dma((NB, 2)),
             dma((STEPS,)),
             dma((STEPS,)),
             dma((8,)),

time: 163 us -> 163 us (level)
  no operation moved by 1% of the time
where the time goes in v4:
time: 163 us
  Pallas kernels  163 us (100%)
    pallas_call x1, Pallas kernels, per_device(): pl.pallas_call(kernel, out_shape=(jax.ShapeDtypeStruct((FFH, D), F32), ja...  155 us
    pallas_call x1, Pallas kernels, per_device(): pl.pallas_call(finish, out_shape=(jax.ShapeDtypeStruct((FFH, D), BF16), j...  7.47 us

profile of v4, /device:TPU:1, one launch (start us, length us, event | category | flops | bytes accessed | tf_op | source)
XLA Modules:
  0.0 163.2 jit_solution(3031666645413672115)
XLA Ops:
  0.6 155.1 %shard_map.76 = (f32[512,3584]{1,0:T(8,128)}, bf16[2048,512]{1,0:T(8,128)(2,1)}, f32[8,128]{1,0:T(8,128)}, f32[8,128]{1,0:T(8,128)}) custom-call(bf16[128,3584]{1,0:T(8,128)(2,1)} %tok_hbm.1, s32[8,128]{1,0:T(8,128)} %bitcast.3, bf16[8,128]{1,0:T(8,128)(2,1)} %bitcast.4, bf16[512,3584]{1,0:T(8,128)(2,1)} %w_hbm.1, bf16[2048,512]{1,0:T(8,128)(2,1)} %act_hbm.1), custom_call_target="tpu_custom_call" | custom-call | tf_op jit(solution)/shard_map/pallas_call | solution.py:632
  155.7 7.5 %shard_map.77 = (bf16[512,3584]{1,0:T(8,128)(2,1)}, bf16[2048,512]{1,0:T(8,128)(2,1)}, f32[8,128]{1,0:T(8,128)}) custom-call(f32[512,3584]{1,0:T(8,128)} %get-tuple-element.10.wg_hbm, bf16[2048,512]{1,0:T(8,128)(2,1)} %get-tuple-element.11.hg_hbm, f32[8,128]{1,0:T(8,128)} %get-tuple-element.12.router_in, f32[8,128]{1,0:T(8,128)} %get-tuple-element.13.factor_ref), custom_call_target="tpu_custom_call" | custom-call | tf_op jit(solution)/shard_map/pallas_call | solution.py:695

commit v5 on v4

--- a/solution.py
+++ b/solution.py
@@ -224,26 +224,22 @@
             gvb, gvr.at[me8], gv_s.at[m], gv_r.at[me8], dev(entry_x(m // 4), m % 4, z, c)
         )
 
-    def z_arrive(k, h):
+    def z_arrive(k, h, part):
         zs = step_z(z, k)
-        for part in range(2):
-            landed(tx.at[zs, h, own_rows, part_cols[part]], zr_r.at[k, h, part])
+        landed(tx.at[zs, h, own_rows, part_cols[part]], zr_r.at[k, h, part])
         odd = lax.rem(k, 2)
         onward = (k <= 4) | ((k == 5) & (h == 0)) | ((k == 6) & (h == 1))
         to_k = k + 2 - k // 6
 
         @pl.when(onward & (odd == 1))
         def _():
-            for part in range(2):
-                zsend(zs, h, part, zr_s.at[k, h, part], zr_r.at[to_k, h, part], 1).start()
+            zsend(zs, h, part, zr_s.at[k, h, part], zr_r.at[to_k, h, part], 1).start()
 
         @pl.when(onward & (odd == 0))
         def _():
-            for part in range(2):
-                zsend(zs, h, part, zr_s.at[k, h, part], zr_r.at[to_k, h, part], -1).start()
-
-        for part in range(2):
-            sib_copy(zs, k, h, part).start()
+            zsend(zs, h, part, zr_s.at[k, h, part], zr_r.at[to_k, h, part], -1).start()
+
+        sib_copy(zs, k, h, part).start()
 
     def row_of(q, i, ys):
         return pl.multiple_of(((q * 2 + i) * 4 + ys) * 16, 16)
@@ -384,25 +380,22 @@
             k, h, side = step_kh(j)
             zs = step_z(z, k)
 
-            @pl.when((k > 0) & (side == 0))
-            def _():
-                z_arrive(k, h)
-
-                @pl.when(k < 7)
-                def _():
-                    z_arrive(k + 1, h)
-
-            for part in range(2):
-                landed(tx.at[zs, h, sib_rows, part_cols[part]], sib_r.at[k, h, part])
-
             @pl.when(j >= NB)
             def _():
                 fh_sent(j - NB)
 
-            gather(j, (0,))
-            fh_start(j, (0, 1))
-            gather(j, (1,))
-            fh_start(j, (2,))
+            for part in range(2):
+                @pl.when((k > 0) & (side == 0))
+                def _(part=part):
+                    z_arrive(k, h, part)
+
+                    @pl.when(k < 7)
+                    def _():
+                        z_arrive(k + 1, h, part)
+
+                landed(tx.at[zs, h, sib_rows, part_cols[part]], sib_r.at[k, h, part])
+                gather(j, (part,))
+                fh_start(j, (0, 1) if part == 0 else (2,))
 
         @pl.when(j == 1)
         def _():

time: 163 us -> 162 us (level)
  Pallas kernels: 163 us -> 161 us
where the time goes in v5:
time: 162 us
  Pallas kernels  161 us (99%)
    pallas_call x1, Pallas kernels, per_device(): pl.pallas_call(kernel, out_shape=(jax.ShapeDtypeStruct((FFH, D), F32), ja...  154 us
    pallas_call x1, Pallas kernels, per_device(): pl.pallas_call(finish, out_shape=(jax.ShapeDtypeStruct((FFH, D), BF16), j...  7.47 us

profile of v5, /device:TPU:1, one launch (start us, length us, event | category | flops | bytes accessed | tf_op | source)
XLA Modules:
  0.0 161.9 jit_solution(15444834864377642189)
XLA Ops:
  0.6 153.8 %shard_map.76 = (f32[512,3584]{1,0:T(8,128)}, bf16[2048,512]{1,0:T(8,128)(2,1)}, f32[8,128]{1,0:T(8,128)}, f32[8,128]{1,0:T(8,128)}) custom-call(bf16[128,3584]{1,0:T(8,128)(2,1)} %tok_hbm.1, s32[8,128]{1,0:T(8,128)} %bitcast.3, bf16[8,128]{1,0:T(8,128)(2,1)} %bitcast.4, bf16[512,3584]{1,0:T(8,128)(2,1)} %w_hbm.1, bf16[2048,512]{1,0:T(8,128)(2,1)} %act_hbm.1), custom_call_target="tpu_custom_call" | custom-call | tf_op jit(solution)/shard_map/pallas_call | solution.py:625
  154.4 7.5 %shard_map.77 = (bf16[512,3584]{1,0:T(8,128)(2,1)}, bf16[2048,512]{1,0:T(8,128)(2,1)}, f32[8,128]{1,0:T(8,128)}) custom-call(f32[512,3584]{1,0:T(8,128)} %get-tuple-element.10.wg_hbm, bf16[2048,512]{1,0:T(8,128)(2,1)} %get-tuple-element.11.hg_hbm, f32[8,128]{1,0:T(8,128)} %get-tuple-element.12.router_in, f32[8,128]{1,0:T(8,128)} %get-tuple-element.13.factor_ref), custom_call_target="tpu_custom_call" | custom-call | tf_op jit(solution)/shard_map/pallas_call | solution.py:688
